TPU v7x, 32 devices: a whole 2x2x4 slice. The times are simulated.
32 devices in a mesh: tm: 8 (over y, x, core), sub: 4 (over z).
Axes of the slice: x: 2, y: 2, z: 4, core: 2. Of those that a mesh axis runs over, the one named last changes fastest.
Arguments:
- feature_maps: bfloat16 [128, 30, 40, 128], P(('tm', 'sub')), may hold values from -6 to 6
- context_maps: bfloat16 [128, 2, 40, 128], P(('tm', 'sub')), may hold values from -6 to 6
- hidden_state: bfloat16 [544, 2, 40, 128], P(('tm', 'sub')), may hold values from -1 to 1
- lookup_grid: int32 [544, 2, 40], P(('tm', 'sub')), may hold values from 41 to 1158, as said below
- loop_edges: int32 [32, 2], P(('tm', 'sub')), may hold values from 0 to 127, as said below
- inverse_depth: float32 [128, 2, 40], P(('tm', 'sub')), may hold values from 0.2 to 2
- translations: float32 [3, 128], replicated, may hold values from -2 to 2
- update_reset_weight: bfloat16 [3, 3, 256, 256], replicated, may hold values from -0.125 to 0.125
- update_reset_bias: float32 [256], replicated, may hold values from -4 to 4
- candidate_weight: bfloat16 [3, 3, 256, 128], replicated, may hold values from -0.125 to 0.125
- candidate_bias: float32 [128], replicated, may hold values from -3 to 3
- correlation_weight: float32 [9, 128], replicated, may hold values from -2 to 2
- flow_weight: float32 [2, 128], replicated, may hold values from -4 to 4
- motion_bias: float32 [128], replicated, may hold values from -3 to 3
- head_weight: bfloat16 [128, 4], replicated, may hold values from -0.5 to 0.5
- head_bias: float32 [4], replicated, may hold values from -3 to 3
Outputs:
- correlation: float32 [544, 9, 2, 40], P(('tm', 'sub'))
- new_hidden: bfloat16 [544, 2, 40, 128], P(('tm', 'sub'))
- revision: float32 [544, 4, 2, 40], P(('tm', 'sub'))
- pose_block: float32 [544, 6, 6], P(('tm', 'sub'))
- pose_gradient: float32 [544, 6], P(('tm', 'sub'))
- depth_pose: float32 [544, 6, 2, 40], P(('tm', 'sub'))
- depth_diagonal: float32 [128, 2, 2, 40], P(('tm', 'sub'))
Inputs may be any that keep to these rules, and one draw needn't show every extreme that they name: `lookup_grid`: each value is a pixel r * 40 + c with 1 <= r <= 28 and 1 <= c <= 38. loop_edges[b, 0] is a keyframe of block b; the targets loop_edges[b, 1] lie anywhere, at most 4 of them in any one block, and some block receives exactly 4.
All inputs are finite; a program needn't handle non-finite values.
Results may differ from a plain program's by a relative error of at most 0.0042.
Values may be sent and summed in bfloat16 or wider, within the bound.
A program may use at most 64 MiB of HBM per device.

v0:
```python
import math

import jax
import jax.numpy as jnp
import numpy as np
from jax import lax
from jax.sharding import PartitionSpec as P

CHANNELS = 128
HIDDEN_SIZE = 128
HEIGHT = 30
WIDTH = 40
KEYFRAMES = 4
QUERY_ROWS = 2
LOOP_MOST = 4


focal = 40.0
highest = lax.Precision.HIGHEST
neighbour_steps = (-2, -1, 1, 2)


def with_halo(shard, sides, width):
    for axis, dim in sides:
        size, length = (lax.axis_size(axis), shard.shape[dim])
        up = [(i, (i + 1) % size) for i in range(size - 1)]
        down = [(j, i) for i, j in up]
        last = lax.slice_in_dim(shard, length - width, length, axis=dim)
        initial = lax.slice_in_dim(shard, 0, width, axis=dim)
        before = lax.ppermute(last, axis, up)
        after = lax.ppermute(initial, axis, down)
        shard = jnp.concatenate([before, shard, after], axis=dim)
    return shard


def window_steps(stride):
    return np.array(
        [row_step * stride + col_step for row_step in (-1, 0, 1) for col_step in (-1, 0, 1)],
        dtype=np.int32,
    )


def conv_taps(values, weight):
    padded = jnp.pad(values, ((0, 0), (1, 1), (1, 1), (0, 0)))
    batch_size, out_rows, out_cols = (values.shape[0], values.shape[1], values.shape[2])
    accumulated = jnp.zeros((batch_size * out_rows * out_cols, weight.shape[-1]), jnp.float32)
    for row_step in range(3):
        for col_step in range(3):
            window = padded[:, row_step : row_step + out_rows, col_step : col_step + out_cols, :]
            accumulated = accumulated + jnp.dot(
                window.reshape(-1, window.shape[-1]),
                weight[row_step, col_step],
                preferred_element_type=jnp.float32,
            )
    return accumulated.reshape(batch_size, out_rows, out_cols, weight.shape[-1])


def look_up(frames_flat, frame_ids, grid_flat, queries, steps, frame_pixels):
    index = frame_ids[:, None, None] * frame_pixels + grid_flat[:, None, :] + steps[None, :, None]
    gathered = frames_flat[index]
    return jnp.einsum("ejqc,eqc->ejq", gathered, queries, preferred_element_type=jnp.float32) * (
        1.0 / math.sqrt(CHANNELS)
    )


def on_device(
    feature_maps,
    context_maps,
    hidden_state,
    lookup_grid,
    loop_edges,
    inverse_depth,
    translations,
    update_reset_weight,
    update_reset_bias,
    candidate_weight,
    candidate_bias,
    correlation_weight,
    flow_weight,
    motion_bias,
    head_weight,
    head_bias,
):
    block_id = lax.axis_index(("tm", "sub"))
    block_total = lax.axis_size(("tm", "sub"))
    near_count = 4 * KEYFRAMES
    edges_block = near_count + 1
    pixels = QUERY_ROWS * WIDTH
    frame_pixels = HEIGHT * WIDTH
    steps_full = jnp.asarray(window_steps(WIDTH))
    near_frame = np.repeat(np.arange(KEYFRAMES), 4).astype(np.int32)
    near_step = np.tile(np.array(neighbour_steps, dtype=np.int32), KEYFRAMES).astype(np.int32)
    first_frame = block_id * KEYFRAMES
    loop_source = loop_edges[0, 0] - first_frame
    source_local = jnp.concatenate([jnp.asarray(near_frame), loop_source[None]])
    source_global = first_frame + source_local
    target_global = jnp.concatenate(
        [first_frame + jnp.asarray(near_frame + near_step), loop_edges[0, 1:2]]
    )
    frame_total = block_total * KEYFRAMES
    valid = ((target_global >= 0) & (target_global < frame_total)).astype(jnp.float32)
    safe_target = jnp.clip(target_global, 0, frame_total - 1)
    query_local = feature_maps[:, :QUERY_ROWS]
    loop_query = lax.dynamic_index_in_dim(query_local, loop_source, 0, keepdims=True)
    loop_grid = lookup_grid[near_count:]
    loop_target = loop_edges[:, 1]
    line_query, line_grid, line_target = (
        lax.all_gather(loop_query, "tm", axis=0, tiled=True),
        lax.all_gather(loop_grid, "tm", axis=0, tiled=True),
        lax.all_gather(loop_target, "tm", axis=0, tiled=True),
    )
    tm_id = lax.axis_index("tm")
    sub_id = lax.axis_index("sub")
    sub_count = lax.axis_size("sub")
    line_ranks = jnp.arange(line_target.shape[0], dtype=jnp.int32)
    line_source = line_ranks * sub_count + sub_id
    target_block = line_target // KEYFRAMES
    to_here = target_block // sub_count == tm_id
    dest_sub = target_block % sub_count
    peers = jnp.arange(sub_count, dtype=jnp.int32)
    matches = to_here[None, :] & (dest_sub[None, :] == peers[:, None])
    within = jnp.cumsum(matches.astype(jnp.int32), axis=1) - 1
    slot_ids = jnp.arange(LOOP_MOST, dtype=jnp.int32)
    picked = matches[:, None, :] & (within[:, None, :] == slot_ids[None, :, None])
    present = jnp.any(picked, axis=2).reshape(-1)
    slot_index = jnp.sum(jnp.where(picked, line_ranks[None, None, :], 0), axis=2).reshape(-1)
    slot_query = jnp.where(
        present[:, None, None, None], line_query[slot_index], jnp.zeros((), jnp.bfloat16)
    )
    slot_grid = line_grid[slot_index]
    slot_source = jnp.where(present, line_source[slot_index], -1)
    slot_target = line_target[slot_index]
    cand_query, cand_grid, cand_source, cand_target = (
        lax.all_to_all(slot_query, "sub", split_axis=0, concat_axis=0, tiled=True),
        lax.all_to_all(slot_grid, "sub", split_axis=0, concat_axis=0, tiled=True),
        lax.all_to_all(slot_source, "sub", split_axis=0, concat_axis=0, tiled=True),
        lax.all_to_all(slot_target, "sub", split_axis=0, concat_axis=0, tiled=True),
    )
    cand_ok = cand_source >= 0
    cand_count = cand_target.shape[0]
    cand_ranks = jnp.arange(cand_count, dtype=jnp.int32)
    order_key = jnp.where(cand_ok, cand_ranks, cand_ranks + cand_count)
    chosen = jnp.argsort(order_key)[:LOOP_MOST]
    chosen_ok = cand_ok[chosen]
    chosen_source = cand_source[chosen]
    chosen_frame = jnp.clip(cand_target[chosen] - first_frame, 0, KEYFRAMES - 1)
    chosen_queries = cand_query[chosen].reshape(LOOP_MOST, pixels, CHANNELS)
    chosen_grid = cand_grid[chosen].reshape(LOOP_MOST, pixels)
    extended = with_halo(feature_maps, ((("tm", "sub"), 0),), 2)
    extended_flat = extended.reshape(-1, CHANNELS)
    near_queries = jnp.repeat(query_local.reshape(KEYFRAMES, pixels, CHANNELS), 4, axis=0)
    near_corr = look_up(
        extended_flat,
        jnp.asarray(near_frame + near_step + 2),
        lookup_grid[:near_count].reshape(near_count, pixels),
        near_queries,
        steps_full,
        frame_pixels,
    ).reshape(near_count, 9, QUERY_ROWS, WIDTH)
    chosen_corr = look_up(
        extended_flat, chosen_frame + 2, chosen_grid, chosen_queries, steps_full, frame_pixels
    )
    all_ranks = jnp.arange(block_total, dtype=jnp.int32)
    one_hot = ((all_ranks[:, None] == chosen_source[None, :]) & chosen_ok[None, :]).astype(
        jnp.float32
    )
    loop_term = jnp.einsum("nl,ljq->njq", one_hot, chosen_corr, precision=highest)
    loop_corr = lax.psum_scatter(loop_term, ("tm", "sub"), scatter_dimension=0, tiled=True).reshape(
        1, 9, QUERY_ROWS, WIDTH
    )
    correlation = jnp.concatenate([near_corr, loop_corr], axis=0) * valid[:, None, None, None]
    col_here = jnp.arange(WIDTH, dtype=jnp.int32)
    row_here = jnp.arange(QUERY_ROWS, dtype=jnp.int32)
    grid_col = lookup_grid % WIDTH
    grid_row = lookup_grid // WIDTH
    flow_u = (grid_col - col_here[None, None, :]).astype(jnp.float32) / focal
    flow_v = (grid_row - row_here[None, :, None]).astype(jnp.float32) / focal
    motion = jax.nn.relu(
        jnp.einsum("ejrc,jh->erch", correlation, correlation_weight, precision=highest)
        + flow_u[..., None] * flow_weight[0]
        + flow_v[..., None] * flow_weight[1]
        + motion_bias
    )
    inputs = (motion + context_maps[source_local].astype(jnp.float32)).astype(jnp.bfloat16)
    joined = jnp.concatenate([hidden_state, inputs], axis=-1)
    gates = jax.nn.sigmoid(conv_taps(joined, update_reset_weight) + update_reset_bias)
    update = gates[..., :HIDDEN_SIZE]
    gated = (gates[..., HIDDEN_SIZE:] * hidden_state.astype(jnp.float32)).astype(jnp.bfloat16)
    candidate = jnp.tanh(
        conv_taps(jnp.concatenate([gated, inputs], axis=-1), candidate_weight) + candidate_bias
    )
    new_hidden = ((1.0 - update) * hidden_state.astype(jnp.float32) + update * candidate).astype(
        jnp.bfloat16
    )
    head = (
        jnp.dot(
            new_hidden.reshape(-1, HIDDEN_SIZE), head_weight, preferred_element_type=jnp.float32
        )
        + head_bias
    )
    head = head.reshape(edges_block, pixels, 4)
    delta_u = head[..., 0]
    delta_v = head[..., 1]
    weight_u = jax.nn.sigmoid(head[..., 2])
    weight_v = jax.nn.sigmoid(head[..., 3])
    revision = jnp.stack([delta_u, delta_v, weight_u, weight_v], axis=1).reshape(
        edges_block, 4, QUERY_ROWS, WIDTH
    )
    pixel_col = jnp.tile(col_here, QUERY_ROWS)
    pixel_row = jnp.repeat(row_here, WIDTH)
    column_coord = (pixel_col.astype(jnp.float32) - (WIDTH - 1) / 2.0) / focal
    row_coord = (pixel_row.astype(jnp.float32) - (HEIGHT - 1) / 2.0) / focal
    depth = inverse_depth[source_local].reshape(edges_block, pixels)
    shift = translations[:, safe_target] - translations[:, source_global]
    shift_x = shift[0][:, None]
    shift_y = shift[1][:, None]
    shift_z = shift[2][:, None]
    col_c = jnp.broadcast_to(column_coord[None, :], (edges_block, pixels))
    row_c = jnp.broadcast_to(row_coord[None, :], (edges_block, pixels))
    flat_col = grid_col.reshape(edges_block, pixels).astype(jnp.float32)
    flat_row = grid_row.reshape(edges_block, pixels).astype(jnp.float32)
    target_u = (flat_col - (WIDTH - 1) / 2.0) / focal + delta_u
    target_v = (flat_row - (HEIGHT - 1) / 2.0) / focal + delta_v
    resid_u = target_u - (col_c + depth * (shift_x - col_c * shift_z))
    resid_v = target_v - (row_c + depth * (shift_y - row_c * shift_z))
    zeros_here = jnp.zeros_like(depth)
    jac_u = jnp.stack(
        [depth, zeros_here, -col_c * depth, -col_c * row_c, 1.0 + col_c * col_c, -row_c]
    )
    jac_v = jnp.stack(
        [zeros_here, depth, -row_c * depth, -(1.0 + row_c * row_c), col_c * row_c, col_c]
    )
    depth_u = shift_x - col_c * shift_z
    depth_v = shift_y - row_c * shift_z
    scaled_u = weight_u * valid[:, None]
    scaled_v = weight_v * valid[:, None]
    pose_block = jnp.einsum(
        "aep,bep->eab", jac_u * scaled_u, jac_u, precision=highest
    ) + jnp.einsum("aep,bep->eab", jac_v * scaled_v, jac_v, precision=highest)
    pose_gradient = jnp.einsum(
        "aep,ep->ea", jac_u * scaled_u, resid_u, precision=highest
    ) + jnp.einsum("aep,ep->ea", jac_v * scaled_v, resid_v, precision=highest)
    depth_pose = (
        (jac_u * (scaled_u * depth_u) + jac_v * (scaled_v * depth_v))
        .transpose(1, 0, 2)
        .reshape(edges_block, 6, QUERY_ROWS, WIDTH)
    )
    curvature = scaled_u * depth_u * depth_u + scaled_v * depth_v * depth_v
    slope = scaled_u * depth_u * resid_u + scaled_v * depth_v * resid_v
    owner = (source_local[:, None] == jnp.arange(KEYFRAMES, dtype=jnp.int32)[None, :]).astype(
        jnp.float32
    )
    depth_diagonal = jnp.stack(
        [
            jnp.einsum("ek,ep->kp", owner, curvature, precision=highest),
            jnp.einsum("ek,ep->kp", owner, slope, precision=highest),
        ],
        axis=1,
    ).reshape(KEYFRAMES, 2, QUERY_ROWS, WIDTH)
    return (
        correlation,
        new_hidden,
        revision,
        pose_block,
        pose_gradient,
        depth_pose,
        depth_diagonal,
    )


def solution(mesh):
    in_specs = (
        P(("tm", "sub"), None, None, None),
        P(("tm", "sub"), None, None, None),
        P(("tm", "sub"), None, None, None),
        P(("tm", "sub"), None, None),
        P(("tm", "sub"), None),
        P(("tm", "sub"), None, None),
        P(),
        P(),
        P(),
        P(),
        P(),
        P(),
        P(),
        P(),
        P(),
        P(),
    )
    out_specs = (
        P(("tm", "sub"), None, None, None),
        P(("tm", "sub"), None, None, None),
        P(("tm", "sub"), None, None, None),
        P(("tm", "sub"), None, None),
        P(("tm", "sub"), None),
        P(("tm", "sub"), None, None, None),
        P(("tm", "sub"), None, None, None),
    )
    return jax.shard_map(
        on_device, mesh=mesh, in_specs=in_specs, out_specs=out_specs, check_vma=False
    )
```

profile of v0, /device:TPU:0, one launch (start us, length us, event | category | flops | bytes accessed | tf_op | source)
XLA Modules:
  0.0 265.0 jit_solution(15001032394547486174)
XLA Ops:
  9.7 1.3 bitcast_dynamic-update-slice_fusion
  11.1 9.5 %all-reduce.2 = s32[8]{0:T(128)S(1)} all-reduce(s32[8]{0:T(128)S(1)} %bitcast_dynamic-update-slice_fusion), channel_id=2, replica_groups=mesh['tm'=8,'sub'=4] {'tm'}, use_global_device_ids=true, to_apply=%add.2 | all-reduce | flops 8 | bytes 64 | tf_op jit(solution)/shard_map/all_gather | solution.py:110
  22.6 4.9 %all-to-all-start = ((s32[4,4,1]{1,2,0:T(1,128)}), s32[4,4,1]{1,2,0:T(1,128)S(1)}, u32[]{:S(2)}, u32[]{:S(2)}) async-start(s32[4,4,1]{1,2,0:T(1,128)} %bitcast.11), calls=%async_computation | async-start | bytes 4096 | tf_op jit(solution)/shard_map/all_to_all | solution.py:136
  27.4 1.4 fusion.109
  28.9 4.1 %collective-permute-start = (bf16[2,30,40,128]{3,2,1,0:T(8,128)(2,1)S(1)}, bf16[2,30,40,128]{3,2,1,0:T(8,128)(2,1)S(1)}, u32[]{:S(2)}, u32[]{:S(2)}) collective-permute-start(bf16[2,30,40,128]{3,2,1,0:T(8,128)(2,1)S(1)} %get-tuple-element.54), channel_id=1, source_target_pairs={{0,1},{1,2},{2,3},{3,4},{4,5},{5,6},{6,7},{7,8},{8,9},{9,10},{10,1... | collective-permute-start | bytes 1843208 | tf_op jit(solution)/shard_map/ppermute | solution.py:30
  39.5 11.8 %all_gather.11 = s32[8,2,40]{2,1,0:T(2,128)S(1)} all-gather(s32[1,2,40]{2,1,0:T(2,128)S(1)} %slice-done), channel_id=1, replica_groups=mesh['tm'=8,'sub'=4] {'tm'}, dimensions={0}, use_global_device_ids=true | all-gather | bytes 2880 | tf_op jit(solution)/shard_map/all_gather | solution.py:109
  52.5 8.0 %all_gather.10 = bf16[8,2,40,128]{3,2,1,0:T(8,128)(2,1)S(1)} all-gather(bf16[1,2,40,128]{3,2,1,0:T(8,128)(2,1)S(1)} %constant_dynamic-slice_fusion), channel_id=1, replica_groups=mesh['tm'=8,'sub'=4] {'tm'}, dimensions={0}, use_global_device_ids=true | all-gather | bytes 184320 | tf_op jit(solution)/shard_map/all_gather | solution.py:108
  61.6 1.4 gather_fusion.11
  71.3 5.5 %all-to-all-start.2 = ((s32[4,4,1]{1,2,0:T(1,128)}), s32[4,4,1]{1,2,0:T(1,128)S(1)}, u32[]{:S(2)}, u32[]{:S(2)}) async-start(s32[4,4,1]{1,2,0:T(1,128)} %bitcast.16), calls=%async_computation.2 | async-start | bytes 4096 | tf_op jit(solution)/shard_map/all_to_all | solution.py:137
  79.4 2.9 %all-to-all-done.2 = s32[4,4,1]{1,2,0:T(1,128)S(1)} async-done(((s32[4,4,1]{1,2,0:T(1,128)}), s32[4,4,1]{1,2,0:T(1,128)S(1)}, u32[]{:S(2)}, u32[]{:S(2)}) %all-to-all-start.2) | async-done | bytes 96 | tf_op jit(solution)/shard_map/all_to_all | solution.py:137
  82.4 3.2 %all-to-all-start.3 = ((s32[4,1,320]{2,1,0:T(1,128)}), s32[4,1,320]{2,1,0:T(1,128)S(1)}, u32[]{:S(2)}, u32[]{:S(2)}) async-start(s32[4,1,320]{2,1,0:T(1,128)} %reshape.1065), calls=%async_computation.3 | async-start | bytes 12288 | tf_op jit(solution)/shard_map/all_to_all | solution.py:135
  89.4 1.8 all-to-all-done.3
  91.2 3.5 %all-to-all-start.1 = ((bf16[16,2,40,128]{3,2,1,0:T(8,128)(2,1)}), bf16[16,2,40,128]{3,2,1,0:T(8,128)(2,1)S(1)}, u32[]{:S(2)}, u32[]{:S(2)}) async-start(bf16[16,2,40,128]{3,2,1,0:T(8,128)(2,1)} %broadcast_select_fusion), calls=%async_computation.1 | async-start | bytes 655360 | tf_op jit(solution)/shard_map/all_to_all | solution.py:134
  97.6 5.9 %all-to-all-done.1 = bf16[16,2,40,128]{3,2,1,0:T(8,128)(2,1)S(1)} async-done(((bf16[16,2,40,128]{3,2,1,0:T(8,128)(2,1)}), bf16[16,2,40,128]{3,2,1,0:T(8,128)(2,1)S(1)}, u32[]{:S(2)}, u32[]{:S(2)}) %all-to-all-start.1) | async-done | bytes 327712 | tf_op jit(solution)/shard_map/all_to_all | solution.py:134
  104.7 1.8 pad_maximum_fusion
  106.5 7.0 %gather_fusion.10 = bf16[2880,128]{1,0:T(8,128)(2,1)S(1)} fusion(bf16[9600,128]{1,0:T(8,128)(2,1)S(1)} %bitcast.215, s32[3072]{0:T(1024)} %pad_clamp_fusion.1), kind=kCustom, calls=%fused_computation.10 | custom fusion | bytes 1486080 | tf_op jit(solution)/shard_map/gather | solution.py:60
  113.5 2.3 fusion.2
  116.8 1.7 fusion.67
  118.5 23.8 %gather_fusion = bf16[11520,128]{1,0:T(8,128)(2,1)} fusion(bf16[9600,128]{1,0:T(8,128)(2,1)S(1)} %bitcast.216, s32[12288]{0:T(1024)S(1)} %pad_clamp_fusion), kind=kCustom, calls=%fused_computation | custom fusion | bytes 5944320 | tf_op jit(solution)/shard_map/gather | solution.py:60
  142.4 4.7 %fusion = f32[16,80,1,9]{3,2,1,0:T(1,128)S(1)} fusion(bf16[16,9,80,128]{3,2,1,0:T(8,128)(2,1)} %bitcast.220, bf16[16,80,128,1]{2,1,0,3:T(8,128)(2,1)S(1)} %bitcast.241), kind=kOutput, calls=%fused_computation.15 | convolution fusion | flops 2949120 | bytes 3322880 | tf_op jit(solution)/shard_map/ejqc,eqc->ejq/dot_general | solution.py:61
  147.7 89.9 %all-reduce.6.cloned.1.call-done = f32[32,9,80]{2,0,1:T(8,128)} async-done(((f32[32,9,80]{2,0,1:T(8,128)}), f32[32,9,80]{2,0,1:T(8,128)}) %all-reduce.6.cloned.1.call-update) | async-done | bytes 92176
  239.3 1.6 fusion.8
  241.0 1.5 pad_slice_fusion.8
  246.7 1.7 pad_slice_fusion
  (228 shorter events, 48.4 us)
Async XLA Ops:
  7.2 54.4 %copy-start = (bf16[4,2,40,128]{3,2,1,0:T(8,128)(2,1)S(1)}, bf16[4,2,40,128]{3,2,1,0:T(8,128)(2,1)}, u32[]{:S(2)}) copy-start(bf16[4,2,40,128]{3,2,1,0:T(8,128)(2,1)} %param.21) | copy-start | bytes 245764
  22.6 48.8 %all-to-all-start = ((s32[4,4,1]{1,2,0:T(1,128)}), s32[4,4,1]{1,2,0:T(1,128)S(1)}, u32[]{:S(2)}, u32[]{:S(2)}) async-start(s32[4,4,1]{1,2,0:T(1,128)} %bitcast.11), calls=%async_computation | async-start | bytes 4096 | tf_op jit(solution)/shard_map/all_to_all | solution.py:136
  28.8 32.3 %copy-start.30 = (s32[16]{0:T(128)S(1)}, s32[16]{0:T(128)}, u32[]{:S(2)}) copy-start(s32[16]{0:T(128)} %constant.142.clone) | copy-start | bytes 196
  28.8 32.4 %slice-start.1 = ((s32[17,2,40]{2,1,0:T(2,128)}), s32[16,2,40]{2,1,0:T(2,128)S(1)}, s32[]{:S(2)}) async-start(s32[17,2,40]{2,1,0:T(2,128)} %param.23), calls=%async_computation.6 | async-start | bytes 32768 | tf_op jit(solution)/shard_map/slice | solution.py:155
  28.9 32.4 %copy-start.26 = (s32[16]{0:T(128)S(1)}, s32[16]{0:T(128)}, u32[]{:S(2)}) copy-start(s32[16]{0:T(128)} %constant.154) | copy-start | bytes 196
  28.9 32.5 %copy-start.17 = (s32[9]{0:T(128)S(1)}, s32[9]{0:T(128)}, u32[]{:S(2)}) copy-start(s32[9]{0:T(128)} %constant.140.clone) | copy-start | bytes 112
  28.9 75.8 %collective-permute-start = (bf16[2,30,40,128]{3,2,1,0:T(8,128)(2,1)S(1)}, bf16[2,30,40,128]{3,2,1,0:T(8,128)(2,1)S(1)}, u32[]{:S(2)}, u32[]{:S(2)}) collective-permute-start(bf16[2,30,40,128]{3,2,1,0:T(8,128)(2,1)S(1)} %get-tuple-element.54), channel_id=1, source_target_pairs={{0,1},{1,2},{2,3},{3,4},{4,5},{5,6},{6,7},{7,8},{8,9},{9,10},{10,1... | collective-permute-start | bytes 1843208 | tf_op jit(solution)/shard_map/ppermute | solution.py:30
  33.0 71.7 %collective-permute-start.1 = (bf16[2,30,40,128]{3,2,1,0:T(8,128)(2,1)S(1)}, bf16[2,30,40,128]{3,2,1,0:T(8,128)(2,1)}, u32[]{:S(2)}, u32[]{:S(2)}) collective-permute-start(bf16[2,30,40,128]{3,2,1,0:T(8,128)(2,1)S(1)} %get-tuple-element.55), channel_id=1, source_target_pairs={{1,0},{2,1},{3,2},{4,3},{5,4},{6,5},{7,6},{8,7},{9,8},{10,9},{11,1... | collective-permute-start | bytes 1843208 | tf_op jit(solution)/shard_map/ppermute | solution.py:31
  35.0 28.6 %copy-start.23 = (f32[2,128]{1,0:T(2,128)S(1)}, f32[2,128]{1,0:T(2,128)}, u32[]{:S(2)}) copy-start(f32[2,128]{1,0:T(2,128)} %param.32) | copy-start | bytes 3076
  35.0 29.1 %copy-start.20 = (f32[3,128]{1,0:T(4,128)S(1)}, f32[3,128]{1,0:T(4,128)}, u32[]{:S(2)}) copy-start(f32[3,128]{1,0:T(4,128)} %param.26) | copy-start | bytes 4612
  66.9 24.2 %copy-start.15 = (f32[80]{0:T(128)}, f32[80]{0:T(128)S(1)}, u32[]{:S(2)}) copy-start(f32[80]{0:T(128)S(1)} %div.169) | copy-start | bytes 964
  71.3 11.0 %all-to-all-start.2 = ((s32[4,4,1]{1,2,0:T(1,128)}), s32[4,4,1]{1,2,0:T(1,128)S(1)}, u32[]{:S(2)}, u32[]{:S(2)}) async-start(s32[4,4,1]{1,2,0:T(1,128)} %bitcast.16), calls=%async_computation.2 | async-start | bytes 4096 | tf_op jit(solution)/shard_map/all_to_all | solution.py:137
  82.4 8.8 %all-to-all-start.3 = ((s32[4,1,320]{2,1,0:T(1,128)}), s32[4,1,320]{2,1,0:T(1,128)S(1)}, u32[]{:S(2)}, u32[]{:S(2)}) async-start(s32[4,1,320]{2,1,0:T(1,128)} %reshape.1065), calls=%async_computation.3 | async-start | bytes 12288 | tf_op jit(solution)/shard_map/all_to_all | solution.py:135
  91.2 12.4 %all-to-all-start.1 = ((bf16[16,2,40,128]{3,2,1,0:T(8,128)(2,1)}), bf16[16,2,40,128]{3,2,1,0:T(8,128)(2,1)S(1)}, u32[]{:S(2)}, u32[]{:S(2)}) async-start(bf16[16,2,40,128]{3,2,1,0:T(8,128)(2,1)} %broadcast_select_fusion), calls=%async_computation.1 | async-start | bytes 655360 | tf_op jit(solution)/shard_map/all_to_all | solution.py:134
  94.6 143.0 %all-reduce.6.cloned.1.call-start = ((), (), s32[]{:S(2)}) async-start(), calls=%async_computation.4 | async-start | bytes 294912
  142.4 96.1 %copy-start.19 = (f32[17]{0:T(128)S(1)}, f32[17]{0:T(128)}, u32[]{:S(2)}) copy-start(f32[17]{0:T(128)} %and_convert_fusion) | copy-start | bytes 208
  147.1 92.2 %copy-start.5 = (bf16[17,2,40,128]{3,2,1,0:T(8,128)(2,1)S(1)}, bf16[17,2,40,128]{3,2,1,0:T(8,128)(2,1)}, u32[]{:S(2)}) copy-start(bf16[17,2,40,128]{3,2,1,0:T(8,128)(2,1)} %gather_fusion.11) | copy-start | bytes 1044484
  147.1 92.2 %copy-start.11 = (f32[17,2,40]{2,1,0:T(2,128)S(1)}, f32[17,2,40]{2,1,0:T(2,128)}, u32[]{:S(2)}) copy-start(f32[17,2,40]{2,1,0:T(2,128)} %get-tuple-element.77) | copy-start | bytes 16324
  147.1 92.2 %copy-start.12 = (f32[17,2,40]{2,1,0:T(2,128)S(1)}, f32[17,2,40]{2,1,0:T(2,128)}, u32[]{:S(2)}) copy-start(f32[17,2,40]{2,1,0:T(2,128)} %convert_multiply_fusion.2) | copy-start | bytes 16324
  147.1 92.2 %copy-start.28 = (f32[128]{0:T(128)S(1)}, f32[128]{0:T(128)}, u32[]{:S(2)}) copy-start(f32[128]{0:T(128)} %get-tuple-element.82) | copy-start | bytes 1540
  147.1 92.2 %copy-start.29 = (f32[128]{0:T(128)S(1)}, f32[128]{0:T(128)}, u32[]{:S(2)}) copy-start(f32[128]{0:T(128)} %get-tuple-element.83) | copy-start | bytes 1540
  147.1 92.2 %copy-start.31 = (f32[9,128]{1,0:T(8,128)S(1)}, f32[9,128]{1,0:T(8,128)}, u32[]{:S(2)}) copy-start(f32[9,128]{1,0:T(8,128)} %param.31) | copy-start | bytes 13828
  147.1 92.2 %copy-start.32 = (f32[128]{0:T(128)S(1)}, f32[128]{0:T(128)}, u32[]{:S(2)}) copy-start(f32[128]{0:T(128)} %param.33) | copy-start | bytes 1540
  147.7 93.2 %copy-start.1 = (bf16[17,2,40,128]{3,2,1,0:T(8,128)(2,1)S(1)}, bf16[17,2,40,128]{3,2,1,0:T(8,128)(2,1)}, u32[]{:S(2)}) copy-start(bf16[17,2,40,128]{3,2,1,0:T(8,128)(2,1)} %param.22) | copy-start | bytes 1044484
  (19 other events, 70.5 us)
Sparse Core Ops, SparseCore 0:
  118.7 118.8 all-reduce.5
where the time goes:
time: 268 us; the launch traced here: 265 us
  waiting for transfers between devices  101 us (38%)
  local copies, waits for them, and re-layouts  64.5 us (24%)
  blocking collectives  29.3 us (11%)
  starting transfers between devices  22.7 us (8%)
  matrix products  17.9 us (7%)
  between operations  15.6 us (6%)
  other arithmetic  14.5 us (5%)
    unnamed x2, waiting for transfers between devices  89.9 us
    gather x2, local copies, waits for them, and re-layouts, look_up(): gathered = frames_flat[index]  30.8 us
    all_gather x1, blocking collectives, on_device(): lax.all_gather(loop_grid, 'tm', axis=0, tiled=True)  11.8 us
    all_gather x1, blocking collectives, on_device(): lax.all_gather(loop_target, 'tm', axis=0, tiled=True)  9.48 us
    all_gather x1, blocking collectives, on_device(): lax.all_gather(loop_query, 'tm', axis=0, tiled=True)  8.04 us
    unnamed x78, local copies, waits for them, and re-layouts  7.16 us
    dot_general x2, matrix products, look_up(): jnp.einsum('ejqc,eqc->ejq', gathered, queries, preferred_element_type=jnp...  6.99 us
    dot_general x18, matrix products, conv_taps(): jnp.dot(window.reshape(-1, window.shape[-1]), weight[row_step, col_step],...  6.21 us
  transfers between devices with their start and end apart: 7, of which 4 were waited for; matrix products, arithmetic and copies ran while one was open for 21% of the time, Pallas kernels for 0%

commit v1 on v0

v1 whole, which is shorter than its diff:
```python
import functools
import math

import jax
import jax.numpy as jnp
from jax import lax
from jax.experimental import pallas as pl
from jax.experimental.pallas import tpu as pltpu
from jax.sharding import PartitionSpec as P

HEIGHT = 30
WIDTH = 40
KEYFRAMES = 4
QUERY_ROWS = 2
LOOP_MOST = 4
PIXELS = QUERY_ROWS * WIDTH
FRAME_PIXELS = HEIGHT * WIDTH
NEAR = 4 * KEYFRAMES
EDGES = NEAR + 1
LANES = 128
TAPS = 9
MESH = pl.DeviceIdType.MESH
VMEM = pltpu.VMEM
bf16 = jnp.bfloat16
f32 = jnp.float32
highest = lax.Precision.HIGHEST
neighbour_steps = (-2, -1, 1, 2)

TO_PREV = ((0, 0, 2), (1, 0, 3), (4, 1, 3))
TO_NEXT = ((11, 2, 0), (14, 3, 0), (15, 3, 1))
QUERY_MSG = 2 * PIXELS + 16
LOOP_MSG = PIXELS + 16


def params(collective_id=None):
    return pltpu.CompilerParams(
        collective_id=collective_id,
        has_side_effects=collective_id is not None,
        vmem_limit_bytes=48 * 1024 * 1024,
    )


def places(tm_count, sub_count):
    tm, sub = lax.axis_index("tm"), lax.axis_index("sub")
    block = tm * sub_count + sub
    total = tm_count * sub_count
    after = lax.rem(block + 1, total)
    before = lax.rem(block + total - 1, total)
    coords = lambda b: (b // sub_count, lax.rem(b, sub_count))
    line = [(lax.rem(tm + d, tm_count), sub) for d in range(1, tm_count)]
    column = [(tm, lax.rem(sub + d, sub_count)) for d in range(1, sub_count)]
    return tm, sub, coords(before), coords(after), line, column


def greet(peers):
    barrier = pltpu.get_barrier_semaphore()
    for peer in peers:
        pl.semaphore_signal(barrier, inc=1, device_id=peer, device_id_type=MESH)
    pl.semaphore_wait(barrier, len(peers))


def send(src, dst, send_sem, recv_sem, peer):
    copy = pltpu.make_async_remote_copy(
        src_ref=src, dst_ref=dst, send_sem=send_sem, recv_sem=recv_sem,
        device_id=peer, device_id_type=MESH,
    )
    copy.start()
    return copy


def queries_out(tm_count, sub_count, to_prev, to_next, loop, from_prev, from_next, chosen,
                got_prev, got_next, line, slots, cands, near_sem, line_sem, sub_sem):
    tm, sub, before, after, line_peers, column = places(tm_count, sub_count)
    greet([before, after] + line_peers + column)
    line_copies = [
        send(loop, line.at[d + 1], line_sem.at[0, d], line_sem.at[1, d], peer)
        for d, peer in enumerate(line_peers)
    ]
    near_copies = [
        send(to_next, got_prev, near_sem.at[0, 0], near_sem.at[1, 0], after),
        send(to_prev, got_next, near_sem.at[0, 1], near_sem.at[1, 1], before),
    ]
    line[0] = loop[...]
    slots[...] = jnp.zeros_like(slots)
    here = tm.astype(f32)
    subs = [lax.rem(sub + e, sub_count).astype(f32) for e in range(sub_count)]
    for copy in line_copies:
        copy.wait()

    def pick(d, counts):
        message = line[d]
        facts = message[PIXELS:].astype(f32)
        mine = facts[2:3] == here
        new = []
        for e in range(sub_count):
            match = (mine & (facts[3:4] == subs[e])).astype(f32)
            for k in range(LOOP_MOST):
                take = jnp.where(counts[e] == float(k), match, 0.0)
                slots[e, k] += (message.astype(f32) * take).astype(bf16)
            new.append(counts[e] + match)
        return tuple(new)

    zero = jnp.zeros((1, LANES), f32)
    lax.fori_loop(0, tm_count, pick, (zero,) * sub_count)
    sub_copies = [
        send(slots.at[e + 1], cands.at[e + 1], sub_sem.at[0, e], sub_sem.at[1, e], peer)
        for e, peer in enumerate(column)
    ]
    cands[0] = slots[0]
    chosen[...] = jnp.zeros_like(chosen)
    for copy in sub_copies:
        copy.wait()

    def compact(e, count):
        for k in range(LOOP_MOST):
            message = cands[e, k].astype(f32)
            there = message[PIXELS + 7 : PIXELS + 8]
            for m in range(LOOP_MOST):
                take = jnp.where(count == float(m), there, 0.0)
                chosen[m] += (message * take).astype(bf16)
            count = count + there
        return count

    lax.fori_loop(0, sub_count, compact, zero)
    for copy in near_copies:
        copy.wait()
    from_prev[...] = got_prev[...]
    from_next[...] = got_next[...]


def results_back(tm_count, sub_count, to_prev, to_next, loops, near_prev, near_next, loop_corr,
                 got_prev, got_next, pool, backs, lines, near_sem, line_sem, sub_sem):
    tm, sub, before, after, line_peers, column = places(tm_count, sub_count)
    greet([before, after] + line_peers + column)
    sub_copies = [
        send(loops, pool.at[e + 1], sub_sem.at[0, e], sub_sem.at[1, e], peer)
        for e, peer in enumerate(column)
    ]
    near_copies = [
        send(to_next, got_prev, near_sem.at[0, 0], near_sem.at[1, 0], after),
        send(to_prev, got_next, near_sem.at[0, 1], near_sem.at[1, 1], before),
    ]
    pool[0] = loops[...]
    backs[...] = jnp.zeros_like(backs)
    own = sub.astype(f32)
    for copy in sub_copies:
        copy.wait()

    def pick(d, carry):
        wanted = lax.rem(tm + d, tm_count).astype(f32)
        for e in range(sub_count):
            for k in range(LOOP_MOST):
                found = pool[e, k]
                match = (found[9:10] == wanted) & (found[10:11] == own)
                backs[d] += found * jnp.where(match, found[11:12], 0.0)
        return carry

    lax.fori_loop(0, tm_count, pick, 0)
    line_copies = [
        send(backs.at[d + 1], lines.at[d + 1], line_sem.at[0, d], line_sem.at[1, d], peer)
        for d, peer in enumerate(line_peers)
    ]
    lines[0] = backs[0]
    for copy in line_copies:
        copy.wait()
    total = lines[0]
    for d in range(1, tm_count):
        total = total + lines[d]
    loop_corr[...] = total
    for copy in near_copies:
        copy.wait()
    near_prev[...] = got_prev[...]
    near_next[...] = got_next[...]


def tap_steps(shape):
    k = lax.broadcasted_iota(jnp.int32, shape, 1)
    row = jnp.where(k >= 6, 1, jnp.where(k >= 3, 0, -1))
    step = row * WIDTH + (k - 3 * (row + 1) - 1)
    return jnp.where(k < TAPS, step, 0)


def correlate(features, queries, grid, from_prev, from_next, chosen, near, to_prev, to_next, loops):
    scale = 1.0 / math.sqrt(features.shape[-1])
    rows = lax.broadcasted_iota(jnp.int32, (16, LANES), 0)

    def split_grid(facts):
        return facts[0:1].astype(f32) * float(WIDTH) + facts[1:2].astype(f32)

    grids = [grid[e : e + 1].astype(f32) for e in range(NEAR)]
    pairs = [[] for _ in range(KEYFRAMES)]
    for i in range(KEYFRAMES):
        for n, step in enumerate(neighbour_steps):
            if 0 <= i + step < KEYFRAMES:
                pairs[i + step].append((queries[i], grids[4 * i + n], near, 4 * i + n))
    for refs, edges, low, out in ((from_prev, TO_NEXT, 2, to_next), (from_next, TO_PREV, 0, to_prev)):
        for n, (_, source, target) in enumerate(edges):
            q = refs[(source - low) * PIXELS : (source - low + 1) * PIXELS]
            facts = refs[2 * PIXELS : 2 * PIXELS + 16].astype(f32)
            pairs[target].append((q, split_grid(facts[2 * n : 2 * n + 2]), out, n))

    def look_up(q, pixel_rows, frame):
        count = len(pixel_rows)
        stacked = jnp.concatenate(pixel_rows + [jnp.zeros((8 - count % 8, LANES), f32)], axis=0)
        columns = jnp.transpose(stacked)
        index = jnp.concatenate(
            [
                jnp.broadcast_to(columns[:PIXELS, n : n + 1], (PIXELS, LANES)).astype(jnp.int32)
                for n in range(count)
            ],
            axis=0,
        )
        index = index + tap_steps(index.shape)
        found = jnp.zeros(index.shape, f32)
        for start in range(0, FRAME_PIXELS, LANES):
            base = min(start, FRAME_PIXELS - LANES)
            part = frame[pl.ds(base, LANES), :]
            volume = lax.dot_general(q, part, (((1,), (1,)), ((), ())), preferred_element_type=f32)
            local = index - base
            inside = (index >= start) & (index < start + LANES)
            picked = jnp.take_along_axis(volume, local & (LANES - 1), axis=1)
            found = jnp.where(inside, picked, found)
        found = found * scale
        return [jnp.transpose(found[n * PIXELS : (n + 1) * PIXELS])[:16] for n in range(count)]

    pad = lambda row: jnp.concatenate([row, jnp.zeros((1, LANES - PIXELS), f32)], axis=1)
    for j in range(KEYFRAMES):
        q = jnp.concatenate([p[0] for p in pairs[j]], axis=0)
        pixel_rows = [p[1] if p[1].shape[1] == LANES else pad(p[1]) for p in pairs[j]]
        for result, (_, _, out, n) in zip(look_up(q, pixel_rows, features.at[j]), pairs[j]):
            out[n, :, :PIXELS] = result
            out[n, :, PIXELS:] = jnp.zeros((16, LANES - PIXELS), f32)

    for k in range(LOOP_MOST):
        facts = chosen[k, PIXELS:].astype(f32)
        frame = jnp.max(facts[4:5]).astype(jnp.int32)
        (result,) = look_up(chosen[k, :PIXELS], [split_grid(facts[0:2])], features.at[frame])
        result = jnp.concatenate([result, jnp.zeros((16, LANES - PIXELS), f32)], axis=1)
        for row, fact in ((9, 5), (10, 6), (11, 7)):
            result = jnp.where(rows == row, jnp.broadcast_to(facts[fact : fact + 1], (16, LANES)), result)
        loops[k] = result


def sigmoid(x):
    return 0.5 * jnp.tanh(0.5 * x) + 0.5


def update(frame_total, near, near_prev, near_next, loop_corr, hidden, context, grid, depth, moves, ends, first_ref,
           gate_weight, gate_bias, cand_weight, cand_bias, enc_weight, head_weight, head_bias,
           correlation, new_hidden, revision, pose, depth_pose, depth_diagonal,
           taps, inputs, heads, sources, shifts):
    first = first_ref[0]
    loop_source = ends[0, 0] - first
    targets, valids = [], []
    for e in range(EDGES):
        if e < NEAR:
            source = first + e // 4
            target = first + e // 4 + neighbour_steps[e % 4]
        else:
            source, target = ends[0, 0], ends[0, 1]
        ok = jnp.where((target >= 0) & (target < frame_total), 1.0, 0.0).astype(f32)
        safe = jnp.clip(target, 0, frame_total - 1)
        for a in range(3):
            shifts[a, e : e + 1, :] = jnp.full((1, LANES), moves[a, safe] - moves[a, source], f32)
        shifts[3, e : e + 1, :] = jnp.full((1, LANES), ok, f32)
        valids.append(ok)
    shift_x, shift_y, shift_z, valid = [shifts[a, :EDGES, :PIXELS] for a in range(4)]

    lane = lax.broadcasted_iota(jnp.int32, (EDGES, PIXELS), 1)
    pixel_row = jnp.where(lane >= WIDTH, 1, 0)
    pixel_col = (lane - WIDTH * pixel_row).astype(f32)
    pixel_row = pixel_row.astype(f32)
    flat = grid[...].astype(f32)
    grid_row = jnp.floor((flat + 0.5) * (1.0 / WIDTH))
    grid_col = flat - float(WIDTH) * grid_row
    flow_u = (grid_col - pixel_col) / 40.0
    flow_v = (grid_row - pixel_row) / 40.0

    crossing = {e: near_next[n] for n, (e, _, _) in enumerate(TO_NEXT)}
    crossing.update({e: near_prev[n] for n, (e, _, _) in enumerate(TO_PREV)})
    low = lax.broadcasted_iota(jnp.int32, (16, PIXELS), 0)
    for e in range(EDGES):
        found = loop_corr[...] if e == NEAR else crossing[e] if e in crossing else near[e]
        found = found[:, :PIXELS] * valids[e]
        correlation[e] = found[:TAPS]
        rows = jnp.where(low < TAPS, found, 0.0)
        rows = jnp.where(low == 9, jnp.broadcast_to(flow_u[e : e + 1], rows.shape), rows)
        rows = jnp.where(low == 10, jnp.broadcast_to(flow_v[e : e + 1], rows.shape), rows)
        rows = jnp.where(low == 11, 1.0, rows)
        motion = lax.dot_general(
            rows, enc_weight[...], (((0,), (0,)), ((), ())), precision=highest, preferred_element_type=f32
        )
        about = context[e // 4 if e < NEAR else loop_source].astype(f32)
        inputs[e] = (jax.nn.relu(motion) + about).astype(bf16).astype(f32)
        sources[e : e + 1, :PIXELS] = depth[pl.ds(e // 4 if e < NEAR else loop_source, 1), :]

    def halves(x):
        return x[:, :WIDTH].reshape(-1, LANES), x[:, WIDTH:].reshape(-1, LANES)

    count = EDGES * WIDTH
    col = lax.broadcasted_iota(jnp.int32, (EDGES, WIDTH, LANES), 1).reshape(count, LANES)

    def around(x):
        left = jnp.where(col == 0, 0.0, pltpu.roll(x, 1, 0))
        right = jnp.where(col == WIDTH - 1, 0.0, pltpu.roll(x, count - 1, 0))
        return left.astype(bf16), x.astype(bf16), right.astype(bf16)

    hid = halves(hidden[...].astype(f32))
    inp = halves(inputs[...])
    for r in range(2):
        for b, value in enumerate(around(hid[r])):
            taps[r, :, 2 * b * LANES : (2 * b + 1) * LANES] = value
        for b, value in enumerate(around(inp[r])):
            taps[r, :, (2 * b + 1) * LANES : (2 * b + 2) * LANES] = value
    dot = functools.partial(jnp.dot, preferred_element_type=f32)
    keep = []
    gated = []
    for r in range(2):
        gates = dot(taps[0], gate_weight[1 - r]) + dot(taps[1], gate_weight[2 - r]) + gate_bias[...]
        gates = sigmoid(gates)
        keep.append(gates[:, :LANES])
        gated.append((gates[:, LANES:] * hid[r]).astype(bf16).astype(f32))
    for r in range(2):
        for b, value in enumerate(around(gated[r])):
            taps[r, :, 2 * b * LANES : (2 * b + 1) * LANES] = value
    both = dot(taps[0], jnp.concatenate([cand_weight[1], cand_weight[0]], axis=1))
    both = both + dot(taps[1], jnp.concatenate([cand_weight[2], cand_weight[1]], axis=1))
    fresh = []
    for r in range(2):
        candidate = jnp.tanh(both[:, r * LANES : (r + 1) * LANES] + cand_bias[...])
        fresh.append(((1.0 - keep[r]) * hid[r] + keep[r] * candidate).reshape(EDGES, WIDTH, LANES))
    new_hidden[...] = jnp.concatenate(fresh, axis=1).astype(bf16)
    for e in range(EDGES):
        head = lax.dot_general(
            head_weight[...], new_hidden[e], (((1,), (1,)), ((), ())), preferred_element_type=f32
        )
        for h in range(4):
            heads[h, e : e + 1, :PIXELS] = head[h : h + 1]
    delta_u = heads[0, :EDGES, :PIXELS] + head_bias[0]
    delta_v = heads[1, :EDGES, :PIXELS] + head_bias[1]
    weight_u = sigmoid(heads[2, :EDGES, :PIXELS] + head_bias[2])
    weight_v = sigmoid(heads[3, :EDGES, :PIXELS] + head_bias[3])
    for h, value in enumerate((delta_u, delta_v, weight_u, weight_v)):
        revision[:, h, :] = value

    d = sources[:EDGES, :PIXELS]
    x = (pixel_col - (WIDTH - 1) / 2.0) / 40.0
    y = (pixel_row - (HEIGHT - 1) / 2.0) / 40.0
    depth_u = shift_x - x * shift_z
    depth_v = shift_y - y * shift_z
    resid_u = (grid_col - (WIDTH - 1) / 2.0) / 40.0 + delta_u - (x + d * depth_u)
    resid_v = (grid_row - (HEIGHT - 1) / 2.0) / 40.0 + delta_v - (y + d * depth_v)
    jac_u = (d, None, -x * d, -x * y, 1.0 + x * x, -y)
    jac_v = (None, d, -y * d, -(1.0 + y * y), x * y, x)
    wu, wv = weight_u * valid, weight_v * valid
    wide = lax.broadcasted_iota(jnp.int32, (EDGES, LANES), 1)
    sums = jnp.zeros((EDGES, LANES), f32)
    zero = jnp.zeros_like(d)

    def both_terms(a, u, v):
        left = zero if jac_u[a] is None or u is None else jac_u[a] * u
        right = zero if jac_v[a] is None or v is None else jac_v[a] * v
        return left + right

    def put(total, value, *where):
        value = jnp.sum(value, axis=1, keepdims=True)
        for k in where:
            total = jnp.where(wide == k, value, total)
        return total

    for a in range(6):
        u = None if jac_u[a] is None else jac_u[a] * wu
        v = None if jac_v[a] is None else jac_v[a] * wv
        for b in range(a, 6):
            sums = put(sums, both_terms(b, u, v), 6 * a + b, 6 * b + a)
        sums = put(sums, both_terms(a, wu * resid_u, wv * resid_v), 36 + a)
        depth_pose[:, a, :] = both_terms(a, wu * depth_u, wv * depth_v)
    pose[...] = sums
    curvature = wu * depth_u * depth_u + wv * depth_v * depth_v
    slope = wu * depth_u * resid_u + wv * depth_v * resid_v
    for n, value in enumerate((curvature, slope)):
        for i in range(KEYFRAMES):
            extra = jnp.where(loop_source == i, value[NEAR:], 0.0)
            depth_diagonal[i, n : n + 1, :] = (
                jnp.sum(value[4 * i : 4 * i + 4], axis=0, keepdims=True) + extra
            )


def on_device(tm_count, sub_count, feature_maps, context_maps, hidden_state, lookup_grid, loop_edges,
              inverse_depth, translations, update_reset_weight, update_reset_bias, candidate_weight,
              candidate_bias, correlation_weight, flow_weight, motion_bias, head_weight, head_bias):
    tm, sub = lax.axis_index("tm"), lax.axis_index("sub")
    first = (tm * sub_count + sub) * KEYFRAMES
    frame_total = tm_count * sub_count * KEYFRAMES
    channels = feature_maps.shape[-1]
    queries = feature_maps[:, :QUERY_ROWS].reshape(KEYFRAMES, PIXELS, channels)
    grid = lookup_grid.reshape(EDGES, PIXELS)
    wide = jnp.pad(grid, ((0, 0), (0, LANES - PIXELS)))
    high, low = (wide // WIDTH).astype(bf16), (wide % WIDTH).astype(bf16)

    def message(low_frame, edges):
        facts = [row for e, _, _ in edges for row in (high[e], low[e])]
        facts += [jnp.zeros((LANES,), bf16)] * (16 - len(facts))
        q = queries[low_frame : low_frame + 2].reshape(2 * PIXELS, channels)
        return jnp.concatenate([q, jnp.stack(facts)], axis=0)

    target = loop_edges[0, 1]
    target_block = target // KEYFRAMES
    numbers = (target_block // sub_count, target_block % sub_count, target % KEYFRAMES, tm, sub, 1)
    facts = [high[NEAR], low[NEAR]]
    facts += [jnp.full((LANES,), n).astype(bf16) for n in numbers]
    facts += [jnp.zeros((LANES,), bf16)] * (16 - len(facts))
    loop_query = lax.dynamic_index_in_dim(queries, loop_edges[0, 0] - first, 0, keepdims=False)
    loop_message = jnp.concatenate([loop_query, jnp.stack(facts)], axis=0)
    to_prev, to_next = message(0, TO_PREV), message(2, TO_NEXT)

    shape = jax.ShapeDtypeStruct
    whole = pl.BlockSpec(memory_space=VMEM)
    scalar = pl.BlockSpec(memory_space=pltpu.SMEM)
    dma = pltpu.SemaphoreType.DMA
    near_msg = (QUERY_MSG, LANES)
    loop_msg = (LOOP_MSG, LANES)
    from_prev, from_next, chosen = pl.pallas_call(
        functools.partial(queries_out, tm_count, sub_count),
        out_shape=(shape(near_msg, bf16), shape(near_msg, bf16), shape((LOOP_MOST,) + loop_msg, bf16)),
        in_specs=[whole] * 3,
        out_specs=(whole,) * 3,
        scratch_shapes=[
            VMEM(near_msg, bf16), VMEM(near_msg, bf16), VMEM((tm_count,) + loop_msg, bf16),
            VMEM((sub_count, LOOP_MOST) + loop_msg, bf16), VMEM((sub_count, LOOP_MOST) + loop_msg, bf16),
            dma((2, 2)), dma((2, tm_count)), dma((2, sub_count)),
        ],
        compiler_params=params(0),
        name="queries_out",
    )(to_prev, to_next, loop_message)

    tap_shape = (16, LANES)
    near, res_prev, res_next, loops = pl.pallas_call(
        correlate,
        out_shape=tuple(shape((n,) + tap_shape, f32) for n in (NEAR, 3, 3, LOOP_MOST)),
        in_specs=[whole] * 6,
        out_specs=(whole,) * 4,
        compiler_params=params(),
        name="correlate",
    )(feature_maps.reshape(KEYFRAMES, FRAME_PIXELS, channels), queries, grid, from_prev, from_next, chosen)

    near_prev, near_next, loop_corr = pl.pallas_call(
        functools.partial(results_back, tm_count, sub_count),
        out_shape=(shape((3,) + tap_shape, f32), shape((3,) + tap_shape, f32), shape(tap_shape, f32)),
        in_specs=[whole] * 3,
        out_specs=(whole,) * 3,
        scratch_shapes=[
            VMEM((3,) + tap_shape, f32), VMEM((3,) + tap_shape, f32),
            VMEM((sub_count, LOOP_MOST) + tap_shape, f32),
            VMEM((tm_count,) + tap_shape, f32), VMEM((tm_count,) + tap_shape, f32),
            dma((2, 2)), dma((2, tm_count)), dma((2, sub_count)),
        ],
        compiler_params=params(1),
        name="results_back",
    )(res_next, res_prev, loops)

    enc_weight = jnp.concatenate(
        [correlation_weight, flow_weight, motion_bias[None], jnp.zeros((4, LANES), f32)], axis=0
    )
    head_rows = jnp.concatenate([head_weight.T, jnp.zeros((12, LANES), bf16)], axis=0)
    correlation, new_hidden, revision, pose, depth_pose, depth_diagonal = pl.pallas_call(
        functools.partial(update, frame_total),
        out_shape=(
            shape((EDGES, TAPS, PIXELS), f32), shape((EDGES, PIXELS, LANES), bf16),
            shape((EDGES, 4, PIXELS), f32), shape((EDGES, LANES), f32),
            shape((EDGES, 6, PIXELS), f32), shape((KEYFRAMES, 2, PIXELS), f32),
        ),
        in_specs=[whole] * 8 + [scalar] * 3 + [whole] * 6 + [scalar],
        out_specs=(whole,) * 6,
        scratch_shapes=[
            VMEM((2, EDGES * WIDTH, 6 * LANES), bf16), VMEM((EDGES, PIXELS, LANES), f32),
            VMEM((4, 24, LANES), f32), VMEM((24, LANES), f32), VMEM((4, 24, LANES), f32),
        ],
        compiler_params=params(),
        name="update",
    )(
        near, near_prev, near_next, loop_corr, hidden_state.reshape(EDGES, PIXELS, LANES),
        context_maps.reshape(KEYFRAMES, PIXELS, LANES), grid, inverse_depth.reshape(KEYFRAMES, PIXELS),
        translations, loop_edges, first[None],
        update_reset_weight.reshape(3, 6 * LANES, 2 * LANES), update_reset_bias[None],
        candidate_weight.reshape(3, 6 * LANES, LANES), candidate_bias[None], enc_weight, head_rows, head_bias,
    )
    split = lambda a: a.reshape(a.shape[:-1] + (QUERY_ROWS, WIDTH))
    return (
        split(correlation), new_hidden.reshape(hidden_state.shape), split(revision),
        pose[:, :36].reshape(EDGES, 6, 6), pose[:, 36:42], split(depth_pose), split(depth_diagonal),
    )


def solution(mesh):
    lead = ("tm", "sub")
    over = lambda rank: P(lead, *([None] * (rank - 1)))
    in_specs = tuple(over(rank) for rank in (4, 4, 4, 3, 2, 3)) + (P(),) * 10
    out_specs = tuple(over(rank) for rank in (4, 4, 4, 3, 2, 4, 4))
    return jax.shard_map(
        functools.partial(on_device, mesh.shape["tm"], mesh.shape["sub"]),
        mesh=mesh, in_specs=in_specs, out_specs=out_specs, check_vma=False,
    )
```

time: 268 us -> 60.7 us (0.23)
  waiting for transfers between devices: 101 us -> 0 us
  local copies, waits for them, and re-layouts: 64.5 us -> 11.3 us
  Pallas kernels: 0 us -> 43.8 us
  blocking collectives: 29.3 us -> 0 us
  starting transfers between devices: 22.7 us -> 0 us
  matrix products: 17.9 us -> 0 us
  other arithmetic: 14.5 us -> 0.89 us
  between operations: 15.6 us -> 4.21 us
    unnamed x2 -> x0, waiting for transfers between devices: 89.9 us -> none
    pallas_call x0 -> x4, Pallas kernels: none -> 43.8 us  [the longest x1 19.4 us: on_device(): pl.pallas_call(functools.partial(queries_out, tm_count, sub_count), out_s...]
    gather x16 -> x0, local copies, waits for them, and re-layouts: 41.2 us -> none  [the longest x2 30.8 us: look_up(): gathered = frames_flat[index]]
    all_gather x3 -> x0, blocking collectives: 29.3 us -> none  [the longest x1 11.8 us: on_device(): lax.all_gather(loop_grid, 'tm', axis=0, tiled=True)]
    dot_general x29 -> x0, matrix products: 17.9 us -> none  [the longest x2 6.99 us: look_up(): jnp.einsum('ejqc,eqc->ejq', gathered, queries, preferred_element_type=jnp...]
    all_to_all x4 -> x0, starting transfers between devices: 17.1 us -> none  [the longest x1 5.53 us: on_device(): lax.all_to_all(slot_target, 'sub', split_axis=0, concat_axis=0, tiled=True)]
    all_to_all x4 -> x0, waiting for transfers between devices: 10.6 us -> none  [the longest x1 5.9 us: on_device(): lax.all_to_all(slot_query, 'sub', split_axis=0, concat_axis=0, tiled=True)]
    ppermute x2 -> x0, starting transfers between devices: 5.39 us -> none  [the longest x1 4.1 us: with_halo(): before = lax.ppermute(last, axis, up)]
  transfers between devices with their start and end apart: 7 -> 0, of which waited for: 4 -> 0; matrix products, arithmetic and copies ran while one was open for 21% -> 0% of each run, Pallas kernels for 0% -> 0%
where the time goes in v1:
time: 60.7 us; the launch traced here: 60.3 us
  Pallas kernels  43.8 us (72%)
  local copies, waits for them, and re-layouts  11.3 us (19%)
  between operations  4.21 us (7%)
  other arithmetic  0.89 us (1%)
    pallas_call x1, Pallas kernels, on_device(): pl.pallas_call(functools.partial(queries_out, tm_count, sub_count), out_s...  19.4 us
    pallas_call x1, Pallas kernels, on_device(): pl.pallas_call(functools.partial(results_back, tm_count, sub_count), out_...  11.3 us
    pallas_call x1, Pallas kernels, on_device(): pl.pallas_call(correlate, out_shape=tuple((shape((n,) + tap_shape, f32) f...  8.02 us
    pallas_call x1, Pallas kernels, on_device(): pl.pallas_call(functools.partial(update, frame_total), out_shape=(shape((...  5.08 us
    reshape x4, local copies, waits for them, and re-layouts, on_device(): split = lambda a: a.reshape(a.shape[:-1] + (QUERY_ROWS, WIDTH))  2.98 us
    unnamed x21, local copies, waits for them, and re-layouts  2 us
    slice x1, local copies, waits for them, and re-layouts, on_device(): target = loop_edges[0, 1]  1.31 us

profile of v1, /device:TPU:0, one launch (start us, length us, event | category | flops | bytes accessed | tf_op | source)
XLA Modules:
  0.0 60.3 jit_solution(292025373163316547)
XLA Ops:
  0.7 0.1 pad.9.clone
  0.8 1.3 %fusion.6 = (s32[1,1]{1,0:T(1,128)}, s32[1,1]{1,0:T(1,128)}) fusion(s32[1,2]{1,0:T(1,128)} %ends.1), kind=kLoop, calls=%fused_computation.12 | loop fusion | bytes 16 | tf_op jit(solution)/shard_map/slice | solution.py:407
  5.5 0.8 %reshape.73.depth = f32[4,80]{1,0:T(4,128)S(1)} reshape(f32[4,2,40]{2,1,0:T(2,128)} %param.21) | data formatting | bytes 2560 | tf_op jit(solution)/shard_map/reshape | solution.py:483
  6.2 0.7 %concatenate.19.head_weight = bf16[16,128]{1,0:T(8,128)(2,1)S(1)} pad(bf16[4,128]{1,0:T(4,128)(2,1)} %bitcast.33, bf16[]{:T(256)} %constant.67.clone.1), padding=0_12x0_0 | pad | bytes 5122 | tf_op jit(solution)/shard_map/concatenate | solution.py:465
  6.9 0.9 %maximum_maximum_fusion.enc_weight = f32[16,128]{1,0:T(8,128)S(1)} fusion(f32[1,128]{1,0:T(1,128)} %bitcast.34, f32[2,128]{1,0:T(2,128)} %param.28, f32[9,128]{1,0:T(8,128)} %param.27, f32[16]{0:T(128)S(1)} %pad.9.clone), kind=kLoop, calls=%fused_computation.8 | loop fusion | flops 6144 | bytes 14400 | tf_op jit(solution)/shard_map/concatenate | solution.py:462
  7.8 0.8 %reshape.68.grid = s32[17,80]{1,0:T(8,128)S(1)} reshape(s32[17,2,40]{2,1,0:T(2,128)} %param.19) | data formatting | bytes 10880 | tf_op jit(solution)/shard_map/reshape | solution.py:397
  8.6 0.9 %slice.67 = bf16[4,2,40,128]{3,2,1,0:T(8,128)(2,1)S(1)} slice(bf16[4,30,40,128]{3,2,1,0:T(8,128)(2,1)} %param.16), slice={[0:4], [0:2], [0:40], [0:128]} | slice | bytes 163840 | tf_op jit(solution)/shard_map/slice | solution.py:396
  9.6 0.1 concatenate.17.loop
  9.6 0.8 %fusion.3 = (bf16[2,2,40,128]{3,2,1,0:T(8,128)(2,1)S(1)}, bf16[2,2,40,128]{3,2,1,0:T(8,128)(2,1)S(1)}) fusion(bf16[4,30,40,128]{3,2,1,0:T(8,128)(2,1)} %param.16), kind=kLoop, calls=%fused_computation.9 | loop fusion | bytes 163840 | tf_op jit(solution)/shard_map/slice | solution.py:404
  10.4 0.1 concatenate.15.to_prev
  10.5 0.1 concatenate.16.to_next
  10.6 19.4 %queries_out.1 = (bf16[176,128]{1,0:T(8,128)(2,1)S(1)}, bf16[176,128]{1,0:T(8,128)(2,1)S(1)}, bf16[4,96,128]{2,1,0:T(8,128)(2,1)S(1)}) custom-call(bf16[176,128]{1,0:T(8,128)(2,1)S(1)} %concatenate.15.to_prev, bf16[176,128]{1,0:T(8,128)(2,1)S(1)} %concatenate.16.to_next, bf16[96,128]{1,0:T(8,128)(2,1)S(1)} %concatenate.17.loop), custom_call_target="tpu_custom_call" | custom-call | tf_op jit(solution)/shard_map/queries_out/pallas_call | solution.py:423
  30.0 1.3 %copy-done = bf16[4,30,40,128]{3,2,1,0:T(8,128)(2,1)S(1)} copy-done((bf16[4,30,40,128]{3,2,1,0:T(8,128)(2,1)S(1)}, bf16[4,30,40,128]{3,2,1,0:T(8,128)(2,1)}, u32[]{:S(2)}) %copy-start) | copy-done | bytes 1228824
  31.3 8.0 %correlate.1 = (f32[16,16,128]{2,1,0:T(8,128)S(1)}, f32[3,16,128]{2,1,0:T(8,128)S(1)}, f32[3,16,128]{2,1,0:T(8,128)S(1)}, f32[4,16,128]{2,1,0:T(8,128)S(1)}) custom-call(bf16[4,1200,128]{2,1,0:T(8,128)(2,1)S(1)} %bitcast.21, bf16[4,80,128]{2,1,0:T(8,128)(2,1)S(1)} %bitcast.25, s32[17,80]{1,0:T(8,128)S(1)} %reshape.68.grid, ...), custom_call_target="tpu_custom_call" | custom-call | tf_op jit(solution)/shard_map/correlate/pallas_call | solution.py:438
  39.3 11.3 %results_back.1 = (f32[3,16,128]{2,1,0:T(8,128)S(1)}, f32[3,16,128]{2,1,0:T(8,128)S(1)}, f32[16,128]{1,0:T(8,128)S(1)}) custom-call(f32[3,16,128]{2,1,0:T(8,128)S(1)} %get-tuple-element.27.to_prev, f32[3,16,128]{2,1,0:T(8,128)S(1)} %get-tuple-element.28.to_next, f32[4,16,128]{2,1,0:T(8,128)S(1)} %get-tuple-element.29.loops), custom_call_target="tpu_custom_call" | custom-call | tf_op jit(solution)/shard_map/results_back/pallas_call | solution.py:447
  50.7 5.1 %update.1 = (f32[17,9,80]{2,1,0:T(8,128)S(1)}, bf16[17,80,128]{2,1,0:T(8,128)(2,1)}, f32[17,4,80]{2,1,0:T(4,128)S(1)}, f32[17,128]{1,0:T(8,128)S(1)}, f32[17,6,80]{2,1,0:T(8,128)S(1)}, /*index=5*/f32[4,2,80]{2,1,0:T(2,128)S(1)}) custom-call(f32[16,16,128]{2,1,0:T(8,128)S(1)} %get-tuple-element.26.near, f32[3,16,128]{2,1,0:T(8,128)S(1)} %get-tuple-element.30.near_prev, ...), custom_call_target="tpu_custom_call" | custom-call | tf_op jit(solution)/shard_map/update/pallas_call | solution.py:466
  55.8 0.7 %reshape.81 = f32[4,2,2,40]{3,2,1,0:T(2,128)} reshape(f32[4,2,80]{2,1,0:T(2,128)S(1)} %get-tuple-element.38) | data formatting | bytes 5120 | tf_op jit(solution)/shard_map/reshape | solution.py:488
  56.5 0.1 slice.87
  56.6 0.7 %copy.28 = f32[17,6]{0,1:T(8,128)} copy(f32[17,6]{1,0:T(8,128)S(1)} %slice.87) | data formatting | bytes 816
  57.3 0.8 %reshape.82 = f32[17,9,2,40]{3,2,1,0:T(2,128)} reshape(f32[17,9,80]{2,1,0:T(8,128)S(1)} %get-tuple-element.33) | data formatting | bytes 97920 | tf_op jit(solution)/shard_map/reshape | solution.py:488
  58.1 0.1 copy.26
  58.2 0.6 %reshape.79 = f32[17,6,6]{0,2,1:T(8,128)} reshape(f32[17,36]{0,1:T(8,128)S(1)} %copy.26) | data formatting | bytes 4896 | tf_op jit(solution)/shard_map/reshape | solution.py:491
  58.8 0.7 %reshape.78 = f32[17,4,2,40]{3,2,1,0:T(2,128)} reshape(f32[17,4,80]{2,1,0:T(4,128)S(1)} %get-tuple-element.35) | data formatting | bytes 43520 | tf_op jit(solution)/shard_map/reshape | solution.py:488
  59.5 0.8 %reshape.80 = f32[17,6,2,40]{3,2,1,0:T(2,128)} reshape(f32[17,6,80]{2,1,0:T(8,128)S(1)} %get-tuple-element.37) | data formatting | bytes 65280 | tf_op jit(solution)/shard_map/reshape | solution.py:488
  (31 shorter events, 0.1 us)
Async XLA Ops:
  4.7 46.0 %copy-start.3 = (bf16[17,2,40,128]{3,2,1,0:T(8,128)(2,1)S(1)}, bf16[17,2,40,128]{3,2,1,0:T(8,128)(2,1)}, u32[]{:S(2)}) copy-start(bf16[17,2,40,128]{3,2,1,0:T(8,128)(2,1)} %param.18) | copy-start | bytes 1044484
  6.9 43.7 %copy-start.2 = (bf16[3,3,256,128]{3,2,1,0:T(8,128)(2,1)S(1)}, bf16[3,3,256,128]{3,2,1,0:T(8,128)(2,1)}, u32[]{:S(2)}) copy-start(bf16[3,3,256,128]{3,2,1,0:T(8,128)(2,1)} %param.25) | copy-start | bytes 1769476
  6.9 43.7 %copy-start.5 = (s32[1,2]{1,0:T(1,128)S(1)}, s32[1,2]{1,0:T(1,128)}, u32[]{:S(2)}) copy-start(s32[1,2]{1,0:T(1,128)} %ends.1) | copy-start | bytes 28
  30.0 1.3 %copy-start = (bf16[4,30,40,128]{3,2,1,0:T(8,128)(2,1)S(1)}, bf16[4,30,40,128]{3,2,1,0:T(8,128)(2,1)}, u32[]{:S(2)}) copy-start(bf16[4,30,40,128]{3,2,1,0:T(8,128)(2,1)} %param.16) | copy-start | bytes 3686404
  31.3 19.4 %copy-start.1 = (bf16[3,3,256,256]{3,2,1,0:T(8,128)(2,1)S(1)}, bf16[3,3,256,256]{3,2,1,0:T(8,128)(2,1)}, u32[]{:S(2)}) copy-start(bf16[3,3,256,256]{3,2,1,0:T(8,128)(2,1)} %param.23) | copy-start | bytes 3538948
  31.3 19.4 %copy-start.4 = (bf16[4,2,40,128]{3,2,1,0:T(8,128)(2,1)S(1)}, bf16[4,2,40,128]{3,2,1,0:T(8,128)(2,1)}, u32[]{:S(2)}) copy-start(bf16[4,2,40,128]{3,2,1,0:T(8,128)(2,1)} %param.17) | copy-start | bytes 245764
  31.3 19.4 %copy-start.6 = (f32[3,128]{1,0:T(4,128)S(1)}, f32[3,128]{1,0:T(4,128)}, u32[]{:S(2)}) copy-start(f32[3,128]{1,0:T(4,128)} %moves.1) | copy-start | bytes 4612
  31.3 19.4 %copy-start.7 = (f32[256]{0:T(256)S(1)}, f32[256]{0:T(256)}, u32[]{:S(2)}) copy-start(f32[256]{0:T(256)} %param.24) | copy-start | bytes 3076
  31.3 19.4 %copy-start.8 = (f32[128]{0:T(128)S(1)}, f32[128]{0:T(128)}, u32[]{:S(2)}) copy-start(f32[128]{0:T(128)} %param.26) | copy-start | bytes 1540
  31.3 19.4 %copy-start.9 = (f32[4]{0:T(128)S(1)}, f32[4]{0:T(128)}, u32[]{:S(2)}) copy-start(f32[4]{0:T(128)} %head_bias.1) | copy-start | bytes 52

commit v2 on v1

--- a/solution.py
+++ b/solution.py
@@ -68,64 +68,93 @@
     return copy
 
 
-def queries_out(tm_count, sub_count, to_prev, to_next, loop, from_prev, from_next, chosen,
-                got_prev, got_next, line, slots, cands, near_sem, line_sem, sub_sem):
-    tm, sub, before, after, line_peers, column = places(tm_count, sub_count)
-    greet([before, after] + line_peers + column)
-    line_copies = [
-        send(loop, line.at[d + 1], line_sem.at[0, d], line_sem.at[1, d], peer)
-        for d, peer in enumerate(line_peers)
+def flatten(x):
+    tail = jnp.zeros((x.shape[0], LANES - PIXELS), x.dtype)
+    return jnp.concatenate([x[:, 0, :], x[:, 1, :], tail], axis=1)
+
+
+def split_rows(grid):
+    flat = flatten(grid).astype(f32)
+    high = jnp.floor((flat + 0.5) * (1.0 / WIDTH))
+    return flat, high, flat - float(WIDTH) * high
+
+
+def queries_out(tm_count, sub_count, features, grid, ends, from_prev, from_next, chosen,
+                to_prev, to_next, got_prev, got_next, line, near_sem, sub_sem, line_sem, pair_sem):
+    tm, sub, before, after, _, column = places(tm_count, sub_count)
+    half = tm_count // 2
+    line_peers = [(lax.rem(tm + 2 * d, tm_count), sub) for d in range(1, half)]
+    other = (tm + 1 - 2 * lax.rem(tm, 2), sub)
+    peers = [before, after, other] + line_peers + column
+    barrier = pltpu.get_barrier_semaphore()
+    for peer in peers:
+        pl.semaphore_signal(barrier, inc=1, device_id=peer, device_id_type=MESH)
+
+    _, high, low = split_rows(grid)
+    query = lambda i: features[i].astype(f32).reshape(PIXELS, LANES)
+
+    def facts(rows):
+        return jnp.concatenate(rows + [jnp.zeros((16 - len(rows), LANES), f32)], axis=0)
+
+    target = ends[0, 1]
+    target_block = target // KEYFRAMES
+    numbers = (
+        target_block // sub_count, lax.rem(target_block, sub_count), lax.rem(target, KEYFRAMES), tm, sub
+    )
+    rows = [high[NEAR:], low[NEAR:]] + [jnp.full((1, LANES), n.astype(f32)) for n in numbers]
+    rows += [jnp.ones((1, LANES), f32)]
+    line[0, 0, 0, :PIXELS] = query(lax.rem(ends[0, 0], KEYFRAMES)).astype(bf16)
+    line[0, 0, 0, PIXELS:] = facts(rows).astype(bf16)
+    for out, start, edges in ((to_prev, 0, TO_PREV), (to_next, 2, TO_NEXT)):
+        for n in range(2):
+            out[n * PIXELS : (n + 1) * PIXELS] = query(start + n).astype(bf16)
+        rows = [row for e, _, _ in edges for row in (high[e : e + 1], low[e : e + 1])]
+        out[2 * PIXELS :] = facts(rows).astype(bf16)
+
+    pl.semaphore_wait(barrier, len(peers))
+    sub_copies = [
+        send(line.at[0, 0, 0], line.at[0, 0, e + 1], sub_sem.at[0, e], sub_sem.at[1, e], peer)
+        for e, peer in enumerate(column)
     ]
     near_copies = [
         send(to_next, got_prev, near_sem.at[0, 0], near_sem.at[1, 0], after),
         send(to_prev, got_next, near_sem.at[0, 1], near_sem.at[1, 1], before),
     ]
-    line[0] = loop[...]
-    slots[...] = jnp.zeros_like(slots)
-    here = tm.astype(f32)
-    subs = [lax.rem(sub + e, sub_count).astype(f32) for e in range(sub_count)]
-    for copy in line_copies:
-        copy.wait()
-
-    def pick(d, counts):
-        message = line[d]
-        facts = message[PIXELS:].astype(f32)
-        mine = facts[2:3] == here
-        new = []
-        for e in range(sub_count):
-            match = (mine & (facts[3:4] == subs[e])).astype(f32)
-            for k in range(LOOP_MOST):
-                take = jnp.where(counts[e] == float(k), match, 0.0)
-                slots[e, k] += (message.astype(f32) * take).astype(bf16)
-            new.append(counts[e] + match)
-        return tuple(new)
-
-    zero = jnp.zeros((1, LANES), f32)
-    lax.fori_loop(0, tm_count, pick, (zero,) * sub_count)
-    sub_copies = [
-        send(slots.at[e + 1], cands.at[e + 1], sub_sem.at[0, e], sub_sem.at[1, e], peer)
-        for e, peer in enumerate(column)
-    ]
-    cands[0] = slots[0]
-    chosen[...] = jnp.zeros_like(chosen)
     for copy in sub_copies:
         copy.wait()
-
-    def compact(e, count):
-        for k in range(LOOP_MOST):
-            message = cands[e, k].astype(f32)
-            there = message[PIXELS + 7 : PIXELS + 8]
+    line_copies = [
+        send(line.at[0, 0], line.at[0, d + 1], line_sem.at[0, d], line_sem.at[1, d], peer)
+        for d, peer in enumerate(line_peers)
+    ]
+    pair_copies = [send(line.at[0, 0], line.at[1, 0], pair_sem.at[0, 0], pair_sem.at[1, 0], other)]
+    chosen[...] = jnp.zeros_like(chosen)
+    here, own = tm.astype(f32), sub.astype(f32)
+
+    def take_from(side, d, count):
+        for e in range(sub_count):
+            message = line[side, d, e]
+            about = message[PIXELS:].astype(f32)
+            match = ((about[2:3] == here) & (about[3:4] == own)).astype(f32)
             for m in range(LOOP_MOST):
-                take = jnp.where(count == float(m), there, 0.0)
-                chosen[m] += (message * take).astype(bf16)
-            count = count + there
+                take = jnp.where(count == float(m), match, 0.0).astype(bf16)
+                chosen[m] += message * take
+            count = count + match
         return count
 
-    lax.fori_loop(0, sub_count, compact, zero)
+    count = take_from(0, 0, jnp.zeros((1, LANES), f32))
+    for d in range(1, half):
+        line_copies[d - 1].wait()
+        pair_copies.append(
+            send(line.at[0, d], line.at[1, d], pair_sem.at[0, d], pair_sem.at[1, d], other)
+        )
+        count = take_from(0, d, count)
     for copy in near_copies:
         copy.wait()
     from_prev[...] = got_prev[...]
     from_next[...] = got_next[...]
+    for d in range(half):
+        pair_copies[d].wait()
+        count = take_from(1, d, count)
 
 
 def results_back(tm_count, sub_count, to_prev, to_next, loops, near_prev, near_next, loop_corr,
@@ -141,18 +170,19 @@
         send(to_prev, got_next, near_sem.at[0, 1], near_sem.at[1, 1], before),
     ]
     pool[0] = loops[...]
-    backs[...] = jnp.zeros_like(backs)
     own = sub.astype(f32)
     for copy in sub_copies:
         copy.wait()
 
     def pick(d, carry):
         wanted = lax.rem(tm + d, tm_count).astype(f32)
+        total = jnp.zeros((16, LANES), f32)
         for e in range(sub_count):
             for k in range(LOOP_MOST):
                 found = pool[e, k]
                 match = (found[9:10] == wanted) & (found[10:11] == own)
-                backs[d] += found * jnp.where(match, found[11:12], 0.0)
+                total = total + found * jnp.where(match, found[11:12], 0.0)
+        backs[d] = total
         return carry
 
     lax.fori_loop(0, tm_count, pick, 0)
@@ -160,12 +190,10 @@
         send(backs.at[d + 1], lines.at[d + 1], line_sem.at[0, d], line_sem.at[1, d], peer)
         for d, peer in enumerate(line_peers)
     ]
-    lines[0] = backs[0]
-    for copy in line_copies:
+    total = backs[0]
+    for d, copy in enumerate(line_copies):
         copy.wait()
-    total = lines[0]
-    for d in range(1, tm_count):
-        total = total + lines[d]
+        total = total + lines[d + 1]
     loop_corr[...] = total
     for copy in near_copies:
         copy.wait()
@@ -180,14 +208,16 @@
     return jnp.where(k < TAPS, step, 0)
 
 
-def correlate(features, queries, grid, from_prev, from_next, chosen, near, to_prev, to_next, loops):
+def correlate(features, heads, grid, from_prev, from_next, chosen, near, to_prev, to_next, loops):
     scale = 1.0 / math.sqrt(features.shape[-1])
     rows = lax.broadcasted_iota(jnp.int32, (16, LANES), 0)
 
     def split_grid(facts):
         return facts[0:1].astype(f32) * float(WIDTH) + facts[1:2].astype(f32)
 
-    grids = [grid[e : e + 1].astype(f32) for e in range(NEAR)]
+    flat = flatten(grid).astype(f32)
+    grids = [flat[e : e + 1] for e in range(NEAR)]
+    queries = [heads[i].astype(f32).reshape(PIXELS, LANES).astype(bf16) for i in range(KEYFRAMES)]
     pairs = [[] for _ in range(KEYFRAMES)]
     for i in range(KEYFRAMES):
         for n, step in enumerate(neighbour_steps):
@@ -223,10 +253,9 @@
         found = found * scale
         return [jnp.transpose(found[n * PIXELS : (n + 1) * PIXELS])[:16] for n in range(count)]
 
-    pad = lambda row: jnp.concatenate([row, jnp.zeros((1, LANES - PIXELS), f32)], axis=1)
     for j in range(KEYFRAMES):
         q = jnp.concatenate([p[0] for p in pairs[j]], axis=0)
-        pixel_rows = [p[1] if p[1].shape[1] == LANES else pad(p[1]) for p in pairs[j]]
+        pixel_rows = [p[1] for p in pairs[j]]
         for result, (_, _, out, n) in zip(look_up(q, pixel_rows, features.at[j]), pairs[j]):
             out[n, :, :PIXELS] = result
             out[n, :, PIXELS:] = jnp.zeros((16, LANES - PIXELS), f32)
@@ -245,12 +274,19 @@
     return 0.5 * jnp.tanh(0.5 * x) + 0.5
 
 
-def update(frame_total, near, near_prev, near_next, loop_corr, hidden, context, grid, depth, moves, ends, first_ref,
-           gate_weight, gate_bias, cand_weight, cand_bias, enc_weight, head_weight, head_bias,
-           correlation, new_hidden, revision, pose, depth_pose, depth_diagonal,
-           taps, inputs, heads, sources, shifts):
-    first = first_ref[0]
-    loop_source = ends[0, 0] - first
+def update(tm_count, sub_count, near, near_prev, near_next, loop_corr, hidden, context, grid, depth, moves, ends,
+           gate_weight, gate_bias, cand_weight, cand_bias, corr_weight, flow_weight, motion_bias, head_weight, head_bias,
+           correlation, new_hidden, revision, pose, gradient, depth_pose, depth_diagonal,
+           taps, inputs, heads, sources, shifts, enc_weight):
+    frame_total = tm_count * sub_count * KEYFRAMES
+    first = (lax.axis_index("tm") * sub_count + lax.axis_index("sub")) * KEYFRAMES
+    enc_weight[0:TAPS] = corr_weight[...]
+    enc_weight[TAPS : TAPS + 2] = flow_weight[...]
+    enc_weight[TAPS + 2 : TAPS + 3] = motion_bias[...]
+    enc_weight[TAPS + 3 :] = jnp.zeros((16 - TAPS - 3, LANES), f32)
+    head_rows = jnp.transpose(head_weight[...].astype(f32))
+    head_rows = jnp.concatenate([head_rows, jnp.zeros((12, LANES), f32)], axis=0).astype(bf16)
+    loop_source = lax.rem(ends[0, 0], KEYFRAMES)
     targets, valids = [], []
     for e in range(EDGES):
         if e < NEAR:
@@ -270,9 +306,7 @@
     pixel_row = jnp.where(lane >= WIDTH, 1, 0)
     pixel_col = (lane - WIDTH * pixel_row).astype(f32)
     pixel_row = pixel_row.astype(f32)
-    flat = grid[...].astype(f32)
-    grid_row = jnp.floor((flat + 0.5) * (1.0 / WIDTH))
-    grid_col = flat - float(WIDTH) * grid_row
+    _, grid_row, grid_col = [value[:, :PIXELS] for value in split_rows(grid)]
     flow_u = (grid_col - pixel_col) / 40.0
     flow_v = (grid_row - pixel_row) / 40.0
 
@@ -282,7 +316,8 @@
     for e in range(EDGES):
         found = loop_corr[...] if e == NEAR else crossing[e] if e in crossing else near[e]
         found = found[:, :PIXELS] * valids[e]
-        correlation[e] = found[:TAPS]
+        correlation[e, :, 0, :] = found[:TAPS, :WIDTH]
+        correlation[e, :, 1, :] = found[:TAPS, WIDTH:]
         rows = jnp.where(low < TAPS, found, 0.0)
         rows = jnp.where(low == 9, jnp.broadcast_to(flow_u[e : e + 1], rows.shape), rows)
         rows = jnp.where(low == 10, jnp.broadcast_to(flow_v[e : e + 1], rows.shape), rows)
@@ -292,7 +327,7 @@
         )
         about = context[e // 4 if e < NEAR else loop_source].astype(f32)
         inputs[e] = (jax.nn.relu(motion) + about).astype(bf16).astype(f32)
-        sources[e : e + 1, :PIXELS] = depth[pl.ds(e // 4 if e < NEAR else loop_source, 1), :]
+        sources[e : e + 1] = flatten(depth[pl.ds(e // 4 if e < NEAR else loop_source, 1)])
 
     def halves(x):
         return x[:, :WIDTH].reshape(-1, LANES), x[:, WIDTH:].reshape(-1, LANES)
@@ -332,7 +367,7 @@
     new_hidden[...] = jnp.concatenate(fresh, axis=1).astype(bf16)
     for e in range(EDGES):
         head = lax.dot_general(
-            head_weight[...], new_hidden[e], (((1,), (1,)), ((), ())), preferred_element_type=f32
+            head_rows, new_hidden[e], (((1,), (1,)), ((), ())), preferred_element_type=f32
         )
         for h in range(4):
             heads[h, e : e + 1, :PIXELS] = head[h : h + 1]
@@ -340,8 +375,12 @@
     delta_v = heads[1, :EDGES, :PIXELS] + head_bias[1]
     weight_u = sigmoid(heads[2, :EDGES, :PIXELS] + head_bias[2])
     weight_v = sigmoid(heads[3, :EDGES, :PIXELS] + head_bias[3])
+    def halve(out, n, value):
+        out[:, n, 0, :] = value[:, :WIDTH]
+        out[:, n, 1, :] = value[:, WIDTH:]
+
     for h, value in enumerate((delta_u, delta_v, weight_u, weight_v)):
-        revision[:, h, :] = value
+        halve(revision, h, value)
 
     d = sources[:EDGES, :PIXELS]
     x = (pixel_col - (WIDTH - 1) / 2.0) / 40.0
@@ -353,8 +392,9 @@
     jac_u = (d, None, -x * d, -x * y, 1.0 + x * x, -y)
     jac_v = (None, d, -y * d, -(1.0 + y * y), x * y, x)
     wu, wv = weight_u * valid, weight_v * valid
-    wide = lax.broadcasted_iota(jnp.int32, (EDGES, LANES), 1)
-    sums = jnp.zeros((EDGES, LANES), f32)
+    six = lax.broadcasted_iota(jnp.int32, (EDGES, 6), 1)
+    blocks = [jnp.zeros((EDGES, 6), f32)] * 6
+    slopes = jnp.zeros((EDGES, 6), f32)
     zero = jnp.zeros_like(d)
 
     def both_terms(a, u, v):
@@ -362,87 +402,71 @@
         right = zero if jac_v[a] is None or v is None else jac_v[a] * v
         return left + right
 
-    def put(total, value, *where):
-        value = jnp.sum(value, axis=1, keepdims=True)
-        for k in where:
-            total = jnp.where(wide == k, value, total)
-        return total
+    def put(total, value, k):
+        return jnp.where(six == k, value, total)
 
     for a in range(6):
         u = None if jac_u[a] is None else jac_u[a] * wu
         v = None if jac_v[a] is None else jac_v[a] * wv
         for b in range(a, 6):
-            sums = put(sums, both_terms(b, u, v), 6 * a + b, 6 * b + a)
-        sums = put(sums, both_terms(a, wu * resid_u, wv * resid_v), 36 + a)
-        depth_pose[:, a, :] = both_terms(a, wu * depth_u, wv * depth_v)
-    pose[...] = sums
+            value = jnp.sum(both_terms(b, u, v), axis=1, keepdims=True)
+            blocks[a] = put(blocks[a], value, b)
+            if b > a:
+                blocks[b] = put(blocks[b], value, a)
+        value = jnp.sum(both_terms(a, wu * resid_u, wv * resid_v), axis=1, keepdims=True)
+        slopes = put(slopes, value, a)
+        halve(depth_pose, a, both_terms(a, wu * depth_u, wv * depth_v))
+    for a in range(6):
+        pose[:, a, :] = blocks[a]
+    gradient[...] = slopes
     curvature = wu * depth_u * depth_u + wv * depth_v * depth_v
     slope = wu * depth_u * resid_u + wv * depth_v * resid_v
     for n, value in enumerate((curvature, slope)):
         for i in range(KEYFRAMES):
             extra = jnp.where(loop_source == i, value[NEAR:], 0.0)
-            depth_diagonal[i, n : n + 1, :] = (
-                jnp.sum(value[4 * i : 4 * i + 4], axis=0, keepdims=True) + extra
-            )
+            extra = extra + jnp.sum(value[4 * i : 4 * i + 4], axis=0, keepdims=True)
+            depth_diagonal[i, n, 0:1, :] = extra[:, :WIDTH]
+            depth_diagonal[i, n, 1:2, :] = extra[:, WIDTH:]
 
 
 def on_device(tm_count, sub_count, feature_maps, context_maps, hidden_state, lookup_grid, loop_edges,
               inverse_depth, translations, update_reset_weight, update_reset_bias, candidate_weight,
               candidate_bias, correlation_weight, flow_weight, motion_bias, head_weight, head_bias):
-    tm, sub = lax.axis_index("tm"), lax.axis_index("sub")
-    first = (tm * sub_count + sub) * KEYFRAMES
-    frame_total = tm_count * sub_count * KEYFRAMES
     channels = feature_maps.shape[-1]
-    queries = feature_maps[:, :QUERY_ROWS].reshape(KEYFRAMES, PIXELS, channels)
-    grid = lookup_grid.reshape(EDGES, PIXELS)
-    wide = jnp.pad(grid, ((0, 0), (0, LANES - PIXELS)))
-    high, low = (wide // WIDTH).astype(bf16), (wide % WIDTH).astype(bf16)
-
-    def message(low_frame, edges):
-        facts = [row for e, _, _ in edges for row in (high[e], low[e])]
-        facts += [jnp.zeros((LANES,), bf16)] * (16 - len(facts))
-        q = queries[low_frame : low_frame + 2].reshape(2 * PIXELS, channels)
-        return jnp.concatenate([q, jnp.stack(facts)], axis=0)
-
-    target = loop_edges[0, 1]
-    target_block = target // KEYFRAMES
-    numbers = (target_block // sub_count, target_block % sub_count, target % KEYFRAMES, tm, sub, 1)
-    facts = [high[NEAR], low[NEAR]]
-    facts += [jnp.full((LANES,), n).astype(bf16) for n in numbers]
-    facts += [jnp.zeros((LANES,), bf16)] * (16 - len(facts))
-    loop_query = lax.dynamic_index_in_dim(queries, loop_edges[0, 0] - first, 0, keepdims=False)
-    loop_message = jnp.concatenate([loop_query, jnp.stack(facts)], axis=0)
-    to_prev, to_next = message(0, TO_PREV), message(2, TO_NEXT)
-
     shape = jax.ShapeDtypeStruct
     whole = pl.BlockSpec(memory_space=VMEM)
     scalar = pl.BlockSpec(memory_space=pltpu.SMEM)
     dma = pltpu.SemaphoreType.DMA
     near_msg = (QUERY_MSG, LANES)
     loop_msg = (LOOP_MSG, LANES)
+    half = tm_count // 2
+    heads_spec = pl.BlockSpec(
+        (KEYFRAMES, QUERY_ROWS, WIDTH, channels), lambda i: (0, 0, 0, 0), memory_space=VMEM
+    )
     from_prev, from_next, chosen = pl.pallas_call(
         functools.partial(queries_out, tm_count, sub_count),
+        grid=(1,),
         out_shape=(shape(near_msg, bf16), shape(near_msg, bf16), shape((LOOP_MOST,) + loop_msg, bf16)),
-        in_specs=[whole] * 3,
+        in_specs=[heads_spec, whole, scalar],
         out_specs=(whole,) * 3,
-        scratch_shapes=[
-            VMEM(near_msg, bf16), VMEM(near_msg, bf16), VMEM((tm_count,) + loop_msg, bf16),
-            VMEM((sub_count, LOOP_MOST) + loop_msg, bf16), VMEM((sub_count, LOOP_MOST) + loop_msg, bf16),
-            dma((2, 2)), dma((2, tm_count)), dma((2, sub_count)),
+        scratch_shapes=[VMEM(near_msg, bf16)] * 4 + [
+            VMEM((2, half, sub_count) + loop_msg, bf16),
+            dma((2, 2)), dma((2, sub_count)), dma((2, half)), dma((2, half)),
         ],
         compiler_params=params(0),
         name="queries_out",
-    )(to_prev, to_next, loop_message)
+    )(feature_maps, lookup_grid, loop_edges)
 
     tap_shape = (16, LANES)
     near, res_prev, res_next, loops = pl.pallas_call(
         correlate,
+        grid=(1,),
         out_shape=tuple(shape((n,) + tap_shape, f32) for n in (NEAR, 3, 3, LOOP_MOST)),
-        in_specs=[whole] * 6,
+        in_specs=[whole, heads_spec] + [whole] * 4,
         out_specs=(whole,) * 4,
         compiler_params=params(),
         name="correlate",
-    )(feature_maps.reshape(KEYFRAMES, FRAME_PIXELS, channels), queries, grid, from_prev, from_next, chosen)
+    )(feature_maps.reshape(KEYFRAMES, FRAME_PIXELS, channels), feature_maps, lookup_grid, from_prev, from_next, chosen)
 
     near_prev, near_next, loop_corr = pl.pallas_call(
         functools.partial(results_back, tm_count, sub_count),
@@ -459,36 +483,30 @@
         name="results_back",
     )(res_next, res_prev, loops)
 
-    enc_weight = jnp.concatenate(
-        [correlation_weight, flow_weight, motion_bias[None], jnp.zeros((4, LANES), f32)], axis=0
-    )
-    head_rows = jnp.concatenate([head_weight.T, jnp.zeros((12, LANES), bf16)], axis=0)
-    correlation, new_hidden, revision, pose, depth_pose, depth_diagonal = pl.pallas_call(
-        functools.partial(update, frame_total),
+    correlation, new_hidden, revision, pose, gradient, depth_pose, depth_diagonal = pl.pallas_call(
+        functools.partial(update, tm_count, sub_count),
         out_shape=(
-            shape((EDGES, TAPS, PIXELS), f32), shape((EDGES, PIXELS, LANES), bf16),
-            shape((EDGES, 4, PIXELS), f32), shape((EDGES, LANES), f32),
-            shape((EDGES, 6, PIXELS), f32), shape((KEYFRAMES, 2, PIXELS), f32),
+            shape((EDGES, TAPS, QUERY_ROWS, WIDTH), f32), shape((EDGES, PIXELS, LANES), bf16),
+            shape((EDGES, 4, QUERY_ROWS, WIDTH), f32), shape((EDGES, 6, 6), f32), shape((EDGES, 6), f32),
+            shape((EDGES, 6, QUERY_ROWS, WIDTH), f32), shape((KEYFRAMES, 2, QUERY_ROWS, WIDTH), f32),
         ),
-        in_specs=[whole] * 8 + [scalar] * 3 + [whole] * 6 + [scalar],
-        out_specs=(whole,) * 6,
+        in_specs=[whole] * 8 + [scalar] * 2 + [whole] * 8 + [scalar],
+        out_specs=(whole,) * 7,
         scratch_shapes=[
             VMEM((2, EDGES * WIDTH, 6 * LANES), bf16), VMEM((EDGES, PIXELS, LANES), f32),
-            VMEM((4, 24, LANES), f32), VMEM((24, LANES), f32), VMEM((4, 24, LANES), f32),
+            VMEM((4, 24, LANES), f32), VMEM((24, LANES), f32), VMEM((4, 24, LANES), f32), VMEM((16, LANES), f32),
         ],
         compiler_params=params(),
         name="update",
     )(
         near, near_prev, near_next, loop_corr, hidden_state.reshape(EDGES, PIXELS, LANES),
-        context_maps.reshape(KEYFRAMES, PIXELS, LANES), grid, inverse_depth.reshape(KEYFRAMES, PIXELS),
-        translations, loop_edges, first[None],
+        context_maps.reshape(KEYFRAMES, PIXELS, LANES), lookup_grid, inverse_depth, translations, loop_edges,
         update_reset_weight.reshape(3, 6 * LANES, 2 * LANES), update_reset_bias[None],
-        candidate_weight.reshape(3, 6 * LANES, LANES), candidate_bias[None], enc_weight, head_rows, head_bias,
-    )
-    split = lambda a: a.reshape(a.shape[:-1] + (QUERY_ROWS, WIDTH))
+        candidate_weight.reshape(3, 6 * LANES, LANES), candidate_bias[None], correlation_weight, flow_weight,
+        motion_bias[None], head_weight, head_bias,
+    )
     return (
-        split(correlation), new_hidden.reshape(hidden_state.shape), split(revision),
-        pose[:, :36].reshape(EDGES, 6, 6), pose[:, 36:42], split(depth_pose), split(depth_diagonal),
+        correlation, new_hidden.reshape(hidden_state.shape), revision, pose, gradient, depth_pose, depth_diagonal
     )
 
 

time: 60.7 us -> 47.5 us (0.78)
  local copies, waits for them, and re-layouts: 11.3 us -> 4.95 us
  between operations: 4.21 us -> 0.86 us
  Pallas kernels: 43.8 us -> 41.4 us
  other arithmetic: 0.89 us -> 0 us
    reshape x7 -> x0, local copies, waits for them, and re-layouts: 5.16 us -> none  [the longest x4 2.98 us: on_device(): split = lambda a: a.reshape(a.shape[:-1] + (QUERY_ROWS, WIDTH))]
    slice x6 -> x0, local copies, waits for them, and re-layouts: 3.2 us -> none  [the longest x1 1.31 us: on_device(): target = loop_edges[0, 1]]
    pallas_call x3, Pallas kernels: 32.5 us -> 29.5 us  [the longest x1 16.1 us: on_device(): pl.pallas_call(functools.partial(queries_out, tm_count, sub_count), grid=...]
    unnamed x21 -> x35, local copies, waits for them, and re-layouts: 2 us -> 4.95 us
    concatenate x5 -> x0, local copies, waits for them, and re-layouts: 0.94 us -> none  [the longest x1 0.68 us: on_device(): jnp.concatenate([head_weight.T, jnp.zeros((12, LANES), bf16)], axis=0)]
    concatenate x1 -> x0, other arithmetic: 0.86 us -> none  [on_device(): jnp.concatenate([correlation_weight, flow_weight, motion_bias[None], jnp....]
    pallas_call x1, Pallas kernels: 11.3 us -> 12 us  [on_device(): pl.pallas_call(functools.partial(results_back, tm_count, sub_count), out_...]
where the time goes in v2:
time: 47.5 us; the launch traced here: 47.2 us
  Pallas kernels  41.4 us (87%)
  local copies, waits for them, and re-layouts  4.95 us (10%)
  between operations  0.86 us (2%)
    pallas_call x1, Pallas kernels, on_device(): pl.pallas_call(functools.partial(queries_out, tm_count, sub_count), grid=...  16.1 us
    pallas_call x1, Pallas kernels, on_device(): pl.pallas_call(functools.partial(results_back, tm_count, sub_count), out_...  12 us
    pallas_call x1, Pallas kernels, on_device(): pl.pallas_call(correlate, grid=(1,), out_shape=tuple((shape((n,) + tap_sh...  7.96 us
    pallas_call x1, Pallas kernels, on_device(): pl.pallas_call(functools.partial(update, tm_count, sub_count), out_shape=...  5.36 us
    unnamed x35, local copies, waits for them, and re-layouts  4.95 us

profile of v2, /device:TPU:0, one launch (start us, length us, event | category | flops | bytes accessed | tf_op | source)
XLA Modules:
  0.0 47.2 jit_solution(7849804640882797633)
XLA Ops:
  0.6 0.8 %copy.23.head_weight = bf16[128,4]{1,0:T(8,128)(2,1)S(1)} copy(bf16[128,4]{0,1:T(4,128)(2,1)} %param.30) | data formatting | bytes 2048 | tf_op args[14]
  1.4 1.3 %copy-done = bf16[4,30,40,128]{3,2,1,0:T(8,128)(2,1)S(1)} copy-done((bf16[4,30,40,128]{3,2,1,0:T(8,128)(2,1)S(1)}, bf16[4,30,40,128]{3,2,1,0:T(8,128)(2,1)}, u32[]{:S(2)}) %copy-start) | copy-done | bytes 1228824
  2.7 0.7 %copy-done.4 = s32[17,2,40]{2,1,0:T(2,128)S(1)} copy-done((s32[17,2,40]{2,1,0:T(2,128)S(1)}, s32[17,2,40]{2,1,0:T(2,128)}, u32[]{:S(2)}) %copy-start.4) | copy-done | bytes 5464
  3.5 0.7 %copy-done.9 = s32[1,2]{1,0:T(1,128)S(1)} copy-done((s32[1,2]{1,0:T(1,128)S(1)}, s32[1,2]{1,0:T(1,128)}, u32[]{:S(2)}) %copy-start.9) | copy-done | bytes 32
  4.1 16.1 %queries_out.1 = (bf16[176,128]{1,0:T(8,128)(2,1)S(1)}, bf16[176,128]{1,0:T(8,128)(2,1)S(1)}, bf16[4,96,128]{2,1,0:T(8,128)(2,1)S(1)}) custom-call(bf16[4,30,40,128]{3,2,1,0:T(8,128)(2,1)S(1)} %copy-done, s32[17,2,40]{2,1,0:T(2,128)S(1)} %copy-done.4, s32[1,2]{1,0:T(1,128)S(1)} %copy-done.9), custom_call_target="tpu_custom_call" | custom-call | tf_op jit(solution)/shard_map/queries_out/pallas_call | solution.py:446
  20.3 0.0 copy-start.1
  20.3 0.0 copy-start.2
  20.3 0.0 copy-start.3
  20.3 0.0 copy-start.5
  20.3 0.0 copy-start.6
  20.3 0.0 copy-start.7
  20.3 0.0 copy-start.8
  20.3 0.0 copy-start.10
  20.4 0.0 copy-start.11
  20.4 0.0 copy-start.12
  20.4 0.0 copy-start.13
  20.4 0.0 copy-start.14
  20.4 0.0 copy-start.15
  20.4 8.0 %correlate.1 = (f32[16,16,128]{2,1,0:T(8,128)S(1)}, f32[3,16,128]{2,1,0:T(8,128)S(1)}, f32[3,16,128]{2,1,0:T(8,128)S(1)}, f32[4,16,128]{2,1,0:T(8,128)S(1)}) custom-call(bf16[4,1200,128]{2,1,0:T(8,128)(2,1)S(1)} %bitcast.9, bf16[4,30,40,128]{3,2,1,0:T(8,128)(2,1)S(1)} %copy-done, s32[17,2,40]{2,1,0:T(2,128)S(1)} %copy-done.4, ...), custom_call_target="tpu_custom_call" | custom-call | tf_op jit(solution)/shard_map/correlate/pallas_call | solution.py:461
  28.4 12.0 %results_back.1 = (f32[3,16,128]{2,1,0:T(8,128)S(1)}, f32[3,16,128]{2,1,0:T(8,128)S(1)}, f32[16,128]{1,0:T(8,128)S(1)}) custom-call(f32[3,16,128]{2,1,0:T(8,128)S(1)} %get-tuple-element.28.to_prev, f32[3,16,128]{2,1,0:T(8,128)S(1)} %get-tuple-element.29.to_next, f32[4,16,128]{2,1,0:T(8,128)S(1)} %get-tuple-element.30.loops), custom_call_target="tpu_custom_call" | custom-call | tf_op jit(solution)/shard_map/results_back/pallas_call | solution.py:471
  40.4 0.0 copy-done.1
  40.5 5.4 %update.1 = (f32[17,9,2,40]{3,2,1,0:T(2,128)}, bf16[17,80,128]{2,1,0:T(8,128)(2,1)}, f32[17,4,2,40]{3,2,1,0:T(2,128)}, f32[17,6,6]{2,1,0:T(8,128)S(1)}, f32[17,6...) custom-call(f32[16,16,128]{2,1,0:T(8,128)S(1)} %get-tuple-element.27.near, ...), custom_call_target="tpu_custom_call" | custom-call | tf_op jit(solution)/shard_map/update/pallas_call | solution.py:486
  45.8 0.7 %copy.25 = f32[17,6]{0,1:T(8,128)} copy(f32[17,6]{1,0:T(8,128)S(1)} %get-tuple-element.45) | data formatting | bytes 816
  46.5 0.7 %copy.24 = f32[17,6,6]{0,2,1:T(8,128)} copy(f32[17,6,6]{2,1,0:T(8,128)S(1)} %get-tuple-element.44) | data formatting | bytes 4896
  (15 shorter events, 0.0 us)
Async XLA Ops:
  1.4 1.3 %copy-start = (bf16[4,30,40,128]{3,2,1,0:T(8,128)(2,1)S(1)}, bf16[4,30,40,128]{3,2,1,0:T(8,128)(2,1)}, u32[]{:S(2)}) copy-start(bf16[4,30,40,128]{3,2,1,0:T(8,128)(2,1)} %heads.1) | copy-start | bytes 3686404
  2.7 0.7 %copy-start.4 = (s32[17,2,40]{2,1,0:T(2,128)S(1)}, s32[17,2,40]{2,1,0:T(2,128)}, u32[]{:S(2)}) copy-start(s32[17,2,40]{2,1,0:T(2,128)} %grid.5) | copy-start | bytes 16324
  3.5 0.7 %copy-start.9 = (s32[1,2]{1,0:T(1,128)S(1)}, s32[1,2]{1,0:T(1,128)}, u32[]{:S(2)}) copy-start(s32[1,2]{1,0:T(1,128)} %ends.3) | copy-start | bytes 28
  20.3 20.1 %copy-start.1 = (bf16[3,3,256,256]{3,2,1,0:T(8,128)(2,1)S(1)}, bf16[3,3,256,256]{3,2,1,0:T(8,128)(2,1)}, u32[]{:S(2)}) copy-start(bf16[3,3,256,256]{3,2,1,0:T(8,128)(2,1)} %param.23) | copy-start | bytes 3538948
  20.3 20.1 %copy-start.2 = (bf16[3,3,256,128]{3,2,1,0:T(8,128)(2,1)S(1)}, bf16[3,3,256,128]{3,2,1,0:T(8,128)(2,1)}, u32[]{:S(2)}) copy-start(bf16[3,3,256,128]{3,2,1,0:T(8,128)(2,1)} %param.25) | copy-start | bytes 1769476
  20.3 20.1 %copy-start.3 = (bf16[17,2,40,128]{3,2,1,0:T(8,128)(2,1)S(1)}, bf16[17,2,40,128]{3,2,1,0:T(8,128)(2,1)}, u32[]{:S(2)}) copy-start(bf16[17,2,40,128]{3,2,1,0:T(8,128)(2,1)} %param.18) | copy-start | bytes 1044484
  20.3 20.1 %copy-start.5 = (bf16[4,2,40,128]{3,2,1,0:T(8,128)(2,1)S(1)}, bf16[4,2,40,128]{3,2,1,0:T(8,128)(2,1)}, u32[]{:S(2)}) copy-start(bf16[4,2,40,128]{3,2,1,0:T(8,128)(2,1)} %param.17) | copy-start | bytes 245764
  20.3 20.1 %copy-start.6 = (f32[9,128]{1,0:T(8,128)S(1)}, f32[9,128]{1,0:T(8,128)}, u32[]{:S(2)}) copy-start(f32[9,128]{1,0:T(8,128)} %corr_weight.1) | copy-start | bytes 13828
  20.3 20.1 %copy-start.7 = (f32[4,2,40]{2,1,0:T(2,128)S(1)}, f32[4,2,40]{2,1,0:T(2,128)}, u32[]{:S(2)}) copy-start(f32[4,2,40]{2,1,0:T(2,128)} %depth.1) | copy-start | bytes 3844
  20.3 20.1 %copy-start.8 = (f32[3,128]{1,0:T(4,128)S(1)}, f32[3,128]{1,0:T(4,128)}, u32[]{:S(2)}) copy-start(f32[3,128]{1,0:T(4,128)} %moves.1) | copy-start | bytes 4612
  20.3 20.1 %copy-start.10 = (s32[1,2]{1,0:T(1,128)S(1)}, s32[1,2]{1,0:T(1,128)}, u32[]{:S(2)}) copy-start(s32[1,2]{1,0:T(1,128)} %ends.3) | copy-start | bytes 28
  20.4 20.1 %copy-start.11 = (f32[256]{0:T(256)S(1)}, f32[256]{0:T(256)}, u32[]{:S(2)}) copy-start(f32[256]{0:T(256)} %param.24) | copy-start | bytes 3076
  20.4 20.1 %copy-start.12 = (f32[2,128]{1,0:T(2,128)S(1)}, f32[2,128]{1,0:T(2,128)}, u32[]{:S(2)}) copy-start(f32[2,128]{1,0:T(2,128)} %flow_weight.1) | copy-start | bytes 3076
  20.4 20.1 %copy-start.13 = (f32[128]{0:T(128)S(1)}, f32[128]{0:T(128)}, u32[]{:S(2)}) copy-start(f32[128]{0:T(128)} %param.26) | copy-start | bytes 1540
  20.4 20.1 %copy-start.14 = (f32[128]{0:T(128)S(1)}, f32[128]{0:T(128)}, u32[]{:S(2)}) copy-start(f32[128]{0:T(128)} %param.29) | copy-start | bytes 1540
  20.4 20.1 %copy-start.15 = (f32[4]{0:T(128)S(1)}, f32[4]{0:T(128)}, u32[]{:S(2)}) copy-start(f32[4]{0:T(128)} %head_bias.1) | copy-start | bytes 52

commit v3 on v2

--- a/solution.py
+++ b/solution.py
@@ -284,8 +284,7 @@
     enc_weight[TAPS : TAPS + 2] = flow_weight[...]
     enc_weight[TAPS + 2 : TAPS + 3] = motion_bias[...]
     enc_weight[TAPS + 3 :] = jnp.zeros((16 - TAPS - 3, LANES), f32)
-    head_rows = jnp.transpose(head_weight[...].astype(f32))
-    head_rows = jnp.concatenate([head_rows, jnp.zeros((12, LANES), f32)], axis=0).astype(bf16)
+    head_rows = jnp.concatenate([head_weight[...].astype(f32), jnp.zeros((12, LANES), f32)], axis=0).astype(bf16)
     loop_source = lax.rem(ends[0, 0], KEYFRAMES)
     targets, valids = [], []
     for e in range(EDGES):
@@ -417,8 +416,8 @@
         slopes = put(slopes, value, a)
         halve(depth_pose, a, both_terms(a, wu * depth_u, wv * depth_v))
     for a in range(6):
-        pose[:, a, :] = blocks[a]
-    gradient[...] = slopes
+        pose[a] = jnp.transpose(blocks[a])
+    gradient[...] = jnp.transpose(slopes)
     curvature = wu * depth_u * depth_u + wv * depth_v * depth_v
     slope = wu * depth_u * resid_u + wv * depth_v * resid_v
     for n, value in enumerate((curvature, slope)):
@@ -487,7 +486,7 @@
         functools.partial(update, tm_count, sub_count),
         out_shape=(
             shape((EDGES, TAPS, QUERY_ROWS, WIDTH), f32), shape((EDGES, PIXELS, LANES), bf16),
-            shape((EDGES, 4, QUERY_ROWS, WIDTH), f32), shape((EDGES, 6, 6), f32), shape((EDGES, 6), f32),
+            shape((EDGES, 4, QUERY_ROWS, WIDTH), f32), shape((6, 6, EDGES), f32), shape((6, EDGES), f32),
             shape((EDGES, 6, QUERY_ROWS, WIDTH), f32), shape((KEYFRAMES, 2, QUERY_ROWS, WIDTH), f32),
         ),
         in_specs=[whole] * 8 + [scalar] * 2 + [whole] * 8 + [scalar],
@@ -503,10 +502,11 @@
         context_maps.reshape(KEYFRAMES, PIXELS, LANES), lookup_grid, inverse_depth, translations, loop_edges,
         update_reset_weight.reshape(3, 6 * LANES, 2 * LANES), update_reset_bias[None],
         candidate_weight.reshape(3, 6 * LANES, LANES), candidate_bias[None], correlation_weight, flow_weight,
-        motion_bias[None], head_weight, head_bias,
+        motion_bias[None], head_weight.T, head_bias,
     )
     return (
-        correlation, new_hidden.reshape(hidden_state.shape), revision, pose, gradient, depth_pose, depth_diagonal
+        correlation, new_hidden.reshape(hidden_state.shape), revision, pose.transpose(2, 0, 1), gradient.T,
+        depth_pose, depth_diagonal,
     )
 
 

time: 47.5 us -> 45.3 us (0.954)
  local copies, waits for them, and re-layouts: 4.95 us -> 2.74 us
    unnamed x35 -> x34, local copies, waits for them, and re-layouts: 4.95 us -> 2.74 us
where the time goes in v3:
time: 45.3 us; the launch traced here: 45.1 us
  Pallas kernels  41.5 us (92%)
  local copies, waits for them, and re-layouts  2.74 us (6%)
  between operations  0.88 us (2%)
    pallas_call x1, Pallas kernels, on_device(): pl.pallas_call(functools.partial(queries_out, tm_count, sub_count), grid=...  16.1 us
    pallas_call x1, Pallas kernels, on_device(): pl.pallas_call(functools.partial(results_back, tm_count, sub_count), out_...  12 us
    pallas_call x1, Pallas kernels, on_device(): pl.pallas_call(correlate, grid=(1,), out_shape=tuple((shape((n,) + tap_sh...  7.96 us
    pallas_call x1, Pallas kernels, on_device(): pl.pallas_call(functools.partial(update, tm_count, sub_count), out_shape=...  5.38 us
    unnamed x34, local copies, waits for them, and re-layouts  2.74 us

profile of v3, /device:TPU:0, one launch (start us, length us, event | category | flops | bytes accessed | tf_op | source)
XLA Modules:
  0.0 45.1 jit_solution(3561977000992815293)
XLA Ops:
  0.6 0.0 copy-start
  0.6 1.3 %copy-done = bf16[4,30,40,128]{3,2,1,0:T(8,128)(2,1)S(1)} copy-done((bf16[4,30,40,128]{3,2,1,0:T(8,128)(2,1)S(1)}, bf16[4,30,40,128]{3,2,1,0:T(8,128)(2,1)}, u32[]{:S(2)}) %copy-start) | copy-done | bytes 1228824
  1.9 0.7 %copy-done.4 = s32[17,2,40]{2,1,0:T(2,128)S(1)} copy-done((s32[17,2,40]{2,1,0:T(2,128)S(1)}, s32[17,2,40]{2,1,0:T(2,128)}, u32[]{:S(2)}) %copy-start.4) | copy-done | bytes 5464
  2.6 0.7 %copy-done.9 = s32[1,2]{1,0:T(1,128)S(1)} copy-done((s32[1,2]{1,0:T(1,128)S(1)}, s32[1,2]{1,0:T(1,128)}, u32[]{:S(2)}) %copy-start.9) | copy-done | bytes 32
  3.3 16.1 %queries_out.1 = (bf16[176,128]{1,0:T(8,128)(2,1)S(1)}, bf16[176,128]{1,0:T(8,128)(2,1)S(1)}, bf16[4,96,128]{2,1,0:T(8,128)(2,1)S(1)}) custom-call(bf16[4,30,40,128]{3,2,1,0:T(8,128)(2,1)S(1)} %copy-done, s32[17,2,40]{2,1,0:T(2,128)S(1)} %copy-done.4, s32[1,2]{1,0:T(1,128)S(1)} %copy-done.9), custom_call_target="tpu_custom_call" | custom-call | tf_op jit(solution)/shard_map/queries_out/pallas_call | solution.py:445
  19.4 0.0 copy-start.1
  19.5 0.0 copy-start.2
  19.5 0.0 copy-start.3
  19.5 0.0 copy-start.5
  19.5 0.0 copy-start.6
  19.5 0.0 copy-start.7
  19.5 0.0 copy-start.8
  19.5 0.0 copy-start.10
  19.5 0.0 copy-start.11
  19.6 0.0 copy-start.12
  19.6 0.0 copy-start.13
  19.6 0.0 copy-start.14
  19.6 0.0 copy-start.15
  19.6 0.0 copy-start.16
  19.6 8.0 %correlate.1 = (f32[16,16,128]{2,1,0:T(8,128)S(1)}, f32[3,16,128]{2,1,0:T(8,128)S(1)}, f32[3,16,128]{2,1,0:T(8,128)S(1)}, f32[4,16,128]{2,1,0:T(8,128)S(1)}) custom-call(bf16[4,1200,128]{2,1,0:T(8,128)(2,1)S(1)} %bitcast.12, bf16[4,30,40,128]{3,2,1,0:T(8,128)(2,1)S(1)} %copy-done, s32[17,2,40]{2,1,0:T(2,128)S(1)} %copy-done.4, ...), custom_call_target="tpu_custom_call" | custom-call | tf_op jit(solution)/shard_map/correlate/pallas_call | solution.py:460
  27.6 12.0 %results_back.1 = (f32[3,16,128]{2,1,0:T(8,128)S(1)}, f32[3,16,128]{2,1,0:T(8,128)S(1)}, f32[16,128]{1,0:T(8,128)S(1)}) custom-call(f32[3,16,128]{2,1,0:T(8,128)S(1)} %get-tuple-element.28.to_prev, f32[3,16,128]{2,1,0:T(8,128)S(1)} %get-tuple-element.29.to_next, f32[4,16,128]{2,1,0:T(8,128)S(1)} %get-tuple-element.30.loops), custom_call_target="tpu_custom_call" | custom-call | tf_op jit(solution)/shard_map/results_back/pallas_call | solution.py:470
  39.6 0.0 copy-done.1
  39.6 0.0 copy-done.2
  39.7 5.4 %update.1 = (f32[17,9,2,40]{3,2,1,0:T(2,128)}, bf16[17,80,128]{2,1,0:T(8,128)(2,1)}, f32[17,4,2,40]{3,2,1,0:T(2,128)}, f32[6,6,17]{2,1,0:T(8,128)}, f32[6,17]{1,...) custom-call(f32[16,16,128]{2,1,0:T(8,128)S(1)} %get-tuple-element.27.near, ...), custom_call_target="tpu_custom_call" | custom-call | tf_op jit(solution)/shard_map/update/pallas_call | solution.py:485
  (14 shorter events, 0.0 us)
Async XLA Ops:
  0.6 1.3 %copy-start = (bf16[4,30,40,128]{3,2,1,0:T(8,128)(2,1)S(1)}, bf16[4,30,40,128]{3,2,1,0:T(8,128)(2,1)}, u32[]{:S(2)}) copy-start(bf16[4,30,40,128]{3,2,1,0:T(8,128)(2,1)} %heads.1) | copy-start | bytes 3686404
  1.9 0.7 %copy-start.4 = (s32[17,2,40]{2,1,0:T(2,128)S(1)}, s32[17,2,40]{2,1,0:T(2,128)}, u32[]{:S(2)}) copy-start(s32[17,2,40]{2,1,0:T(2,128)} %grid.5) | copy-start | bytes 16324
  2.6 0.7 %copy-start.9 = (s32[1,2]{1,0:T(1,128)S(1)}, s32[1,2]{1,0:T(1,128)}, u32[]{:S(2)}) copy-start(s32[1,2]{1,0:T(1,128)} %ends.3) | copy-start | bytes 28
  19.4 20.2 %copy-start.1 = (bf16[3,3,256,256]{3,2,1,0:T(8,128)(2,1)S(1)}, bf16[3,3,256,256]{3,2,1,0:T(8,128)(2,1)}, u32[]{:S(2)}) copy-start(bf16[3,3,256,256]{3,2,1,0:T(8,128)(2,1)} %param.23) | copy-start | bytes 3538948
  19.5 20.2 %copy-start.2 = (bf16[3,3,256,128]{3,2,1,0:T(8,128)(2,1)S(1)}, bf16[3,3,256,128]{3,2,1,0:T(8,128)(2,1)}, u32[]{:S(2)}) copy-start(bf16[3,3,256,128]{3,2,1,0:T(8,128)(2,1)} %param.25) | copy-start | bytes 1769476
  19.5 20.2 %copy-start.3 = (bf16[17,2,40,128]{3,2,1,0:T(8,128)(2,1)S(1)}, bf16[17,2,40,128]{3,2,1,0:T(8,128)(2,1)}, u32[]{:S(2)}) copy-start(bf16[17,2,40,128]{3,2,1,0:T(8,128)(2,1)} %param.18) | copy-start | bytes 1044484
  19.5 20.2 %copy-start.5 = (bf16[4,2,40,128]{3,2,1,0:T(8,128)(2,1)S(1)}, bf16[4,2,40,128]{3,2,1,0:T(8,128)(2,1)}, u32[]{:S(2)}) copy-start(bf16[4,2,40,128]{3,2,1,0:T(8,128)(2,1)} %param.17) | copy-start | bytes 245764
  19.5 20.2 %copy-start.6 = (f32[9,128]{1,0:T(8,128)S(1)}, f32[9,128]{1,0:T(8,128)}, u32[]{:S(2)}) copy-start(f32[9,128]{1,0:T(8,128)} %corr_weight.1) | copy-start | bytes 13828
  19.5 20.2 %copy-start.7 = (f32[4,2,40]{2,1,0:T(2,128)S(1)}, f32[4,2,40]{2,1,0:T(2,128)}, u32[]{:S(2)}) copy-start(f32[4,2,40]{2,1,0:T(2,128)} %depth.1) | copy-start | bytes 3844
  19.5 20.1 %copy-start.8 = (f32[3,128]{1,0:T(4,128)S(1)}, f32[3,128]{1,0:T(4,128)}, u32[]{:S(2)}) copy-start(f32[3,128]{1,0:T(4,128)} %moves.1) | copy-start | bytes 4612
  19.5 20.1 %copy-start.10 = (s32[1,2]{1,0:T(1,128)S(1)}, s32[1,2]{1,0:T(1,128)}, u32[]{:S(2)}) copy-start(s32[1,2]{1,0:T(1,128)} %ends.3) | copy-start | bytes 28
  19.5 20.1 %copy-start.11 = (f32[256]{0:T(256)S(1)}, f32[256]{0:T(256)}, u32[]{:S(2)}) copy-start(f32[256]{0:T(256)} %param.24) | copy-start | bytes 3076
  19.6 20.1 %copy-start.12 = (f32[2,128]{1,0:T(2,128)S(1)}, f32[2,128]{1,0:T(2,128)}, u32[]{:S(2)}) copy-start(f32[2,128]{1,0:T(2,128)} %flow_weight.1) | copy-start | bytes 3076
  19.6 20.1 %copy-start.13 = (bf16[128,4]{0,1:T(4,128)(2,1)S(1)}, bf16[128,4]{0,1:T(4,128)(2,1)}, u32[]{:S(2)}) copy-start(bf16[128,4]{0,1:T(4,128)(2,1)} %param.30) | copy-start | bytes 3076
  19.6 20.1 %copy-start.14 = (f32[128]{0:T(128)S(1)}, f32[128]{0:T(128)}, u32[]{:S(2)}) copy-start(f32[128]{0:T(128)} %param.26) | copy-start | bytes 1540
  19.6 20.1 %copy-start.15 = (f32[128]{0:T(128)S(1)}, f32[128]{0:T(128)}, u32[]{:S(2)}) copy-start(f32[128]{0:T(128)} %param.29) | copy-start | bytes 1540
  19.6 20.1 %copy-start.16 = (f32[4]{0:T(128)S(1)}, f32[4]{0:T(128)}, u32[]{:S(2)}) copy-start(f32[4]{0:T(128)} %head_bias.1) | copy-start | bytes 52
